TPU v7x, 32 devices: a whole 2x2x4 slice. The times are simulated.
32 devices in a mesh: expert: 2 (over x), dp: 16 (over z, y, core).
Axes of the slice: x: 2, y: 2, z: 4, core: 2. Of those that a mesh axis runs over, the one named last changes fastest.
Arguments:
- x_rows: bfloat16 [2, 16, 2, 2, 3072], P('expert', 'dp'), may hold values from -6 to 6
- cot_rows: bfloat16 [2, 16, 2, 2, 3072], P('expert', 'dp'), may hold values from -3 to 3
- counts: int32 [2, 16, 2], P(None, 'dp'), may hold values from 0 to 2, as said below
- w_gate: bfloat16 [2, 3072, 2048], P('expert', None, 'dp'), may hold values from -0.109375 to 0.109375
- w_up: bfloat16 [2, 3072, 2048], P('expert', None, 'dp'), may hold values from -0.109375 to 0.109375
- w_down: bfloat16 [2, 2048, 3072], P('expert', 'dp'), may hold values from -0.125 to 0.125
- kept_blocks: int32 [2], P('expert'), may hold values from 4 to 16
- block_rank: int32 [2, 16], P('expert', 'dp'), may hold values from 0 to 15, each once within a row
Outputs:
- grad_rows: bfloat16 [2, 16, 2, 2, 3072], P('expert', 'dp')
- grad_gate: bfloat16 [2, 3072, 2048], P('expert', None, 'dp')
- grad_up: bfloat16 [2, 3072, 2048], P('expert', None, 'dp')
- grad_down: bfloat16 [2, 2048, 3072], P('expert', 'dp')
Inputs may be any that keep to these rules, and one draw needn't show every extreme that they name: The live slots of a source's buffer for an expert are its first ones. For every expert e and index d the sum over sources s of counts[s, d, e] is at most 4, and it equals 4 for every d of some expert.
All inputs are finite; a program needn't handle non-finite values.
Results may differ from a plain program's by a relative error of at most 0.005.
Values may be sent and summed in bfloat16 or wider, within the bound.
A program may use at most 64 MiB of HBM per device.

v0:
```python
import jax
import jax.numpy as jnp
from jax import lax
from jax.sharding import PartitionSpec as P

LIVE = 4


def compact_matrix(slot_counts, live_rows, capacity):
    sources = slot_counts.shape[0]
    within_slot = jnp.tile(jnp.arange(capacity, dtype=jnp.int32), sources)
    count_slot = jnp.repeat(slot_counts, capacity)
    offsets = jnp.repeat(jnp.cumsum(slot_counts) - slot_counts, capacity)
    target = offsets + within_slot
    alive = within_slot < count_slot
    row_index = jnp.arange(live_rows, dtype=jnp.int32)[:, None]
    return ((row_index == target[None, :]) & alive[None, :]).astype(jnp.bfloat16)


def contract(left, right, left_dim, right_dim):
    return lax.dot_general(
        left, right, (((left_dim,), (right_dim,)), ((), ())), preferred_element_type=jnp.float32
    )


def body(x_rows, cot_rows, counts, w_gate, w_up, w_down, kept_blocks, block_rank):
    expert_count = x_rows.shape[2]
    capacity = x_rows.shape[3]
    model_width = x_rows.shape[4]
    slot_rows = x_rows.reshape(expert_count, capacity, model_width)
    slot_cots = cot_rows.reshape(expert_count, capacity, model_width)
    my_expert = lax.axis_index("expert")
    picked = jnp.arange(expert_count, dtype=jnp.int32)[None, :] == my_expert
    own_counts = jnp.sum(jnp.where(picked, counts[:, 0, :], 0), axis=1)
    chooser = compact_matrix(own_counts, LIVE, capacity)

    def pack_rows(received):
        flat_rows = received.reshape(-1, model_width)
        return jnp.dot(chooser, flat_rows, preferred_element_type=jnp.float32).astype(jnp.bfloat16)

    got_rows, got_cots = (
        lax.all_to_all(slot_rows, "expert", split_axis=0, concat_axis=0, tiled=True),
        lax.all_to_all(slot_cots, "expert", split_axis=0, concat_axis=0, tiled=True),
    )
    group_rows, group_cots = (
        lax.all_gather(pack_rows(got_rows), "dp", axis=0, tiled=True),
        lax.all_gather(pack_rows(got_cots), "dp", axis=0, tiled=True),
    )
    gate_weight = w_gate[0]
    up_weight = w_up[0]
    down_weight = w_down[0]
    keep_mask = (block_rank.reshape(()) < kept_blocks.reshape(())).astype(jnp.float32)
    gate_pre = jnp.dot(group_rows, gate_weight, preferred_element_type=jnp.float32)
    up_pre = jnp.dot(group_rows, up_weight, preferred_element_type=jnp.float32)
    sigmoid_gate = jax.nn.sigmoid(gate_pre)
    activated = gate_pre * sigmoid_gate
    hidden = (activated * up_pre * keep_mask).astype(jnp.bfloat16)
    hidden_grad = contract(group_cots, down_weight, 1, 1)
    up_grad = (hidden_grad * activated * keep_mask).astype(jnp.bfloat16)
    gate_grad = (
        hidden_grad * up_pre * sigmoid_gate * (1.0 + gate_pre * (1.0 - sigmoid_gate)) * keep_mask
    ).astype(jnp.bfloat16)
    grad_down = contract(hidden, group_cots, 0, 0).astype(jnp.bfloat16)
    grad_gate = contract(group_rows, gate_grad, 0, 0).astype(jnp.bfloat16)
    grad_up = contract(group_rows, up_grad, 0, 0).astype(jnp.bfloat16)
    whole_term = contract(gate_grad, gate_weight, 1, 1) + contract(up_grad, up_weight, 1, 1)
    row_grads = lax.psum_scatter(whole_term, "dp", scatter_dimension=0, tiled=True)
    row_grads = row_grads.astype(jnp.bfloat16)
    slot_grads = contract(chooser, row_grads, 0, 0).astype(jnp.bfloat16)
    slot_grads = slot_grads.reshape(expert_count, capacity, model_width)
    returned = lax.all_to_all(slot_grads, "expert", split_axis=0, concat_axis=0, tiled=True)
    grad_rows = returned.reshape(1, 1, expert_count, capacity, model_width)
    return (grad_rows, grad_gate[None], grad_up[None], grad_down[None])


def solution(mesh):
    in_specs = (
        P("expert", "dp", None, None, None),
        P("expert", "dp", None, None, None),
        P(None, "dp", None),
        P("expert", None, "dp"),
        P("expert", None, "dp"),
        P("expert", "dp", None),
        P("expert"),
        P("expert", "dp"),
    )
    out_specs = (
        P("expert", "dp", None, None, None),
        P("expert", None, "dp"),
        P("expert", None, "dp"),
        P("expert", "dp", None),
    )
    return jax.shard_map(body, mesh=mesh, in_specs=in_specs, out_specs=out_specs, check_vma=False)
```

profile of v0, /device:TPU:0, one launch (start us, length us, event | category | flops | bytes accessed | tf_op | source)
XLA Modules:
  0.0 137.9 jit_solution(16545698538518222873)
XLA Ops:
  0.6 0.0 copy-start
  0.7 4.3 %all-to-all-start.1 = ((bf16[2,2,3072]{2,1,0:T(2,128)(2,1)}), bf16[2,2,3072]{2,1,0:T(2,128)(2,1)S(1)}, u32[]{:S(2)}, u32[]{:S(2)}) async-start(bf16[2,2,3072]{2,1,0:T(2,128)(2,1)} %bitcast.50), calls=%async_computation.1 | async-start | bytes 49152 | tf_op jit(solution)/shard_map/all_to_all | solution.py:42
  5.0 0.8 select_reduce_fusion
  5.8 0.2 reduce-window.9
  6.0 0.1 iota_add_fusion
  6.1 0.1 iota_compare_fusion.1
  6.1 0.1 add.22
  6.2 0.1 lt.14
  7.6 1.2 dynamic-slice
  9.5 3.3 %all-to-all-start = ((bf16[2,2,3072]{2,1,0:T(2,128)(2,1)}), bf16[2,2,3072]{2,1,0:T(2,128)(2,1)S(1)}, u32[]{:S(2)}, u32[]{:S(2)}) async-start(bf16[2,2,3072]{2,1,0:T(2,128)(2,1)} %bitcast.51), calls=%async_computation | async-start | bytes 49152 | tf_op jit(solution)/shard_map/all_to_all | solution.py:43
  12.8 0.1 fusion.4
  13.0 23.2 %all-gather.1 = bf16[16,4,3072]{2,1,0:T(4,128)(2,1)S(1)} all-gather(bf16[1,4,3072]{2,1,0:T(4,128)(2,1)S(1)} %fusion.4), channel_id=1, replica_groups=mesh['expert'=2,'dp'=16] {'dp'}, dimensions={0}, use_global_device_ids=true | all-gather | bytes 417792 | tf_op jit(solution)/shard_map/all_gather | solution.py:46
  36.2 0.1 reshape.98
  36.3 0.9 fusion.10
  37.2 0.9 fusion.7
  38.1 0.1 fusion.3
  38.2 18.7 %all-gather = bf16[16,4,3072]{2,1,0:T(4,128)(2,1)S(1)} all-gather(bf16[1,4,3072]{2,1,0:T(4,128)(2,1)S(1)} %fusion.3), channel_id=1, replica_groups=mesh['expert'=2,'dp'=16] {'dp'}, dimensions={0}, use_global_device_ids=true | all-gather | bytes 417792 | tf_op jit(solution)/shard_map/all_gather | solution.py:47
  56.9 0.1 reshape.96
  57.0 1.2 multiply_convert_fusion.1
  58.2 0.4 fusion.5
  58.6 0.0 copy-start.3
  58.6 0.0 copy-start.4
  58.6 1.3 fusion
  59.9 1.3 fusion.2
  61.2 0.4 convolution_add_fusion
  61.6 67.7 %all-reduce.2 = bf16[64,3072]{1,0:T(8,128)(2,1)S(1)} all-reduce(f32[64,3072]{1,0:T(8,128)S(1)} %convolution_add_fusion), channel_id=2, replica_groups=mesh['expert'=2,'dp'=16] {'dp'}, use_global_device_ids=true, to_apply=%region_2.3.clone | all-reduce | flops 196608 | bytes 1179648
  129.3 0.2 convolution_convert_fusion.3
  129.5 0.6 reshape.93
  130.1 3.3 %all-to-all-start.2 = ((bf16[2,2,3072]{2,1,0:T(2,128)(2,1)}), bf16[2,2,3072]{2,1,0:T(2,128)(2,1)S(1)}, u32[]{:S(2)}, u32[]{:S(2)}) async-start(bf16[2,2,3072]{2,1,0:T(2,128)(2,1)} %reshape.93), calls=%async_computation.2 | async-start | bytes 49152 | tf_op jit(solution)/shard_map/all_to_all | solution.py:71
  133.4 1.3 fusion.1
  134.7 2.6 %all-to-all-done.2 = bf16[2,2,3072]{2,1,0:T(2,128)(2,1)S(1)} async-done(((bf16[2,2,3072]{2,1,0:T(2,128)(2,1)}), bf16[2,2,3072]{2,1,0:T(2,128)(2,1)S(1)}, u32[]{:S(2)}, u32[]{:S(2)}) %all-to-all-start.2) | async-done | bytes 24608 | tf_op jit(solution)/shard_map/all_to_all | solution.py:71
  137.3 0.6 copy.17
  (21 shorter events, 0.1 us)
Async XLA Ops:
  0.6 36.5 %copy-start = (bf16[1,3072,128]{2,1,0:T(8,128)(2,1)S(1)}, bf16[1,3072,128]{2,1,0:T(8,128)(2,1)}, u32[]{:S(2)}) copy-start(bf16[1,3072,128]{2,1,0:T(8,128)(2,1)} %param.11) | copy-start | bytes 2359300
  0.6 35.6 %copy-start.1 = (bf16[1,3072,128]{2,1,0:T(8,128)(2,1)S(1)}, bf16[1,3072,128]{2,1,0:T(8,128)(2,1)}, u32[]{:S(2)}) copy-start(bf16[1,3072,128]{2,1,0:T(8,128)(2,1)} %param.12) | copy-start | bytes 2359300
  0.7 8.9 %all-to-all-start.1 = ((bf16[2,2,3072]{2,1,0:T(2,128)(2,1)}), bf16[2,2,3072]{2,1,0:T(2,128)(2,1)S(1)}, u32[]{:S(2)}, u32[]{:S(2)}) async-start(bf16[2,2,3072]{2,1,0:T(2,128)(2,1)} %bitcast.50), calls=%async_computation.1 | async-start | bytes 49152 | tf_op jit(solution)/shard_map/all_to_all | solution.py:42
  6.2 31.9 %copy-start.5 = (s32[4]{0:T(128)}, s32[4]{0:T(128)S(1)}, u32[]{:S(2)}) copy-start(s32[4]{0:T(128)S(1)} %add.22) | copy-start | bytes 52
  6.3 31.8 %copy-start.7 = (pred[4]{0:T(512)(128)(4,1)}, pred[4]{0:T(512)(128)(4,1)S(1)}, u32[]{:S(2)}) copy-start(pred[4]{0:T(512)(128)(4,1)S(1)} %lt.14) | copy-start | bytes 16
  9.5 28.5 %all-to-all-start = ((bf16[2,2,3072]{2,1,0:T(2,128)(2,1)}), bf16[2,2,3072]{2,1,0:T(2,128)(2,1)S(1)}, u32[]{:S(2)}, u32[]{:S(2)}) async-start(bf16[2,2,3072]{2,1,0:T(2,128)(2,1)} %bitcast.51), calls=%async_computation | async-start | bytes 49152 | tf_op jit(solution)/shard_map/all_to_all | solution.py:43
  38.1 18.9 %copy-start.2 = (bf16[1,128,3072]{2,1,0:T(8,128)(2,1)S(1)}, bf16[1,128,3072]{2,1,0:T(8,128)(2,1)}, u32[]{:S(2)}) copy-start(bf16[1,128,3072]{2,1,0:T(8,128)(2,1)} %param.13) | copy-start | bytes 2359300
  58.6 1.3 copy-start.3
  58.6 1.3 copy-start.4
  61.6 67.7 %copy-start.6 = (s32[4]{0:T(128)S(1)}, s32[4]{0:T(128)}, u32[]{:S(2)}) copy-start(s32[4]{0:T(128)} %copy-done.5) | copy-start | bytes 52
  61.6 67.7 %copy-start.8 = (pred[4]{0:T(512)(128)(4,1)S(1)}, pred[4]{0:T(512)(128)(4,1)}, u32[]{:S(2)}) copy-start(pred[4]{0:T(512)(128)(4,1)} %copy-done.7) | copy-start | bytes 16
  130.1 7.2 %all-to-all-start.2 = ((bf16[2,2,3072]{2,1,0:T(2,128)(2,1)}), bf16[2,2,3072]{2,1,0:T(2,128)(2,1)S(1)}, u32[]{:S(2)}, u32[]{:S(2)}) async-start(bf16[2,2,3072]{2,1,0:T(2,128)(2,1)} %reshape.93), calls=%async_computation.2 | async-start | bytes 49152 | tf_op jit(solution)/shard_map/all_to_all | solution.py:71
where the time goes:
time: 138 us
  blocking collectives  110 us (80%)
  starting transfers between devices  10.9 us (8%)
  matrix products  8.04 us (6%)
  local copies, waits for them, and re-layouts  2.89 us (2%)
  between operations  2.77 us (2%)
  waiting for transfers between devices  2.62 us (2%)
    unnamed x1, blocking collectives  67.7 us
    all_gather x1, blocking collectives, body(): lax.all_gather(pack_rows(got_rows), 'dp', axis=0, tiled=True)  23.2 us
    all_gather x1, blocking collectives, body(): lax.all_gather(pack_rows(got_cots), 'dp', axis=0, tiled=True)  18.7 us
    dot_general x7, matrix products, contract(): lax.dot_general(left, right, (((left_dim,), (right_dim,)), ((), ())), pre...  6.01 us
    all_to_all x1, starting transfers between devices, body(): lax.all_to_all(slot_rows, 'expert', split_axis=0, concat_axis=0, tiled=True)  4.35 us
    all_to_all x1, starting transfers between devices, body(): lax.all_to_all(slot_cots, 'expert', split_axis=0, concat_axis=0, tiled=True)  3.3 us
    all_to_all x1, starting transfers between devices, body(): lax.all_to_all(slot_grads, 'expert', split_axis=0, concat_axis=0, tiled=T...  3.29 us
  transfers between devices with their start and end apart: 3, of which 1 were waited for; matrix products, arithmetic and copies ran while one was open for 4% of the time, Pallas kernels for 0%

commit v1 on v0

--- a/solution.py
+++ b/solution.py
@@ -1,6 +1,8 @@
 import jax
 import jax.numpy as jnp
 from jax import lax
+from jax.experimental import pallas as pl
+from jax.experimental.pallas import tpu as pltpu
 from jax.sharding import PartitionSpec as P
 
 LIVE = 4
@@ -73,6 +75,295 @@
     return (grad_rows, grad_gate[None], grad_up[None], grad_down[None])
 
 
+def exchange_kernel(
+    prep_ref, counts_ref, kept_ref, rank_ref, wg_ref, wu_ref, wd_ref,
+    rows_out, gate_out, up_out, down_out,
+    stage, landed, rows, w_in, w_down, acc_gu, acc_dh, sib_out, sib_in, part, unit, unit_in,
+    final_out, final_in, grad_in, grad_down,
+    s1_send, s1_recv, z_send, z_recv, y_send, y_recv, sb_send, sb_recv,
+    r1_send, r1_recv, r2_send, r2_recv, f_send, f_recv, load_sem, store_sem,
+):
+    s = lax.axis_index("expert")
+    d = lax.axis_index("dp")
+    z, y, c = d // 4, (d // 2) % 2, d % 2
+    width = rows.shape[1]
+    half = width // 2
+    quarter = half // 4
+    pair = half // 2
+
+    def device(e, zz, yy, cc):
+        return (e, zz * 4 + yy * 2 + cc)
+
+    def remote(src, dst, send, recv, where):
+        return pltpu.make_async_remote_copy(
+            src_ref=src, dst_ref=dst, send_sem=send, recv_sem=recv, device_id=where,
+            device_id_type=pl.DeviceIdType.MESH,
+        )
+
+    near = [(0, 1), (1, 0), (1, 1)]
+    chips = [(dz, dy) for dz in range(4) for dy in range(2) if (dz, dy) != (0, 0)]
+
+    def near_device(de, dc):
+        return device((s + de) % 2, z, y, (c + dc) % 2)
+
+    def chip_device(dz, dy):
+        return device(s, (z + dz) % 4, (y + dy) % 2, c)
+
+    loads = [
+        pltpu.make_async_copy(wg_ref.at[0], w_in.at[:, pl.ds(0, 128)], load_sem.at[0]),
+        pltpu.make_async_copy(wu_ref.at[0], w_in.at[:, pl.ds(128, 128)], load_sem.at[1]),
+        pltpu.make_async_copy(wd_ref.at[0], w_down, load_sem.at[2]),
+    ]
+    barrier = pltpu.get_barrier_semaphore()
+    for de, dc in near:
+        pl.semaphore_signal(barrier, inc=1, device_id=near_device(de, dc), device_id_type=pl.DeviceIdType.MESH)
+    for dz, dy in chips:
+        pl.semaphore_signal(barrier, inc=1, device_id=chip_device(dz, dy), device_id_type=pl.DeviceIdType.MESH)
+    for load in loads:
+        load.start()
+
+    row16 = lax.broadcasted_iota(jnp.int32, (16, quarter), 0)
+    slot = (row16 >> 2) & 1
+    for e in range(2):
+        live = jnp.where(s == 0, counts_ref[0, 0, e], counts_ref[1, 0, e])
+        for h in range(2):
+            value = prep_ref[e, h].astype(jnp.float32)
+            stage[e, h] = jnp.where(slot < live, value, 0.0).astype(jnp.bfloat16)
+
+    i = lax.broadcasted_iota(jnp.int32, (64, 64), 0)
+    j = lax.broadcasted_iota(jnp.int32, (64, 64), 1)
+    order = (
+        ((i >> 4) == (j & 3))
+        & (((i >> 3) & 1) == ((j >> 3) & 1))
+        & (((i >> 2) & 1) == ((j >> 5) & 1))
+        & (((i >> 1) & 1) == ((j >> 4) & 1))
+        & ((i & 1) == ((j >> 2) & 1))
+    ).astype(jnp.float32).astype(jnp.bfloat16)
+    oi = lax.broadcasted_iota(jnp.int32, (16, 64), 0)
+    oj = lax.broadcasted_iota(jnp.int32, (16, 64), 1)
+    chosen = (
+        ((oi >> 3) == (oj >> 5))
+        & (((oi >> 2) & 1) == (oj & 1))
+        & (((oi >> 1) & 1) == ((oj >> 4) & 1))
+        & ((oi & 1) == ((oj >> 3) & 1))
+        & (((oj >> 2) & 1) == c)
+        & (((oj >> 1) & 1) == s)
+    ).astype(jnp.float32).astype(jnp.bfloat16)
+
+    pl.semaphore_wait(barrier, len(near) + len(chips))
+
+    mine = pl.ds(pl.multiple_of((c * 2 + s) * 16, 16), 16)
+    sends = []
+    first = []
+    for de, dc in near:
+        index = de * 2 + dc
+        copy = remote(
+            stage.at[(s + de) % 2, (c + dc) % 2], landed.at[mine, :], s1_send.at[index], s1_recv.at[index],
+            near_device(de, dc),
+        )
+        copy.start()
+        first.append(copy)
+    landed[mine, :] = stage[s, c]
+    for copy in first:
+        copy.wait_recv()
+    sends += first
+
+    def block(zz, yy, hh):
+        return rows.at[
+            pl.ds(pl.multiple_of((yy * 4 + zz) * 16, 16), 16), pl.ds(pl.multiple_of(hh * half, 128), half)
+        ]
+
+    ordered = jnp.dot(order, landed[...], preferred_element_type=jnp.float32).astype(jnp.bfloat16)
+    my_rows = pl.ds(pl.multiple_of((y * 4 + z) * 16, 16), 16)
+    for g in range(4):
+        rows[my_rows, pl.ds(pl.multiple_of(c * half + g * quarter, 128), quarter)] = ordered[g * 16:(g + 1) * 16, :]
+
+    def forward(ref, send, recv, where):
+        copy = remote(ref, ref, send, recv, where)
+        copy.start()
+        sends.append(copy)
+        return copy
+
+    sibling = device(s, z, y, 1 - c)
+    opposite = device(s, z, 1 - y, c)
+    own = block(z, y, c)
+    z_copies = {}
+    for dz in (2, 1, 3):
+        z_copies[dz] = forward(own, z_send.at[dz - 1], z_recv.at[dz - 1], device(s, (z + dz) % 4, y, c))
+    y_copies = [forward(own, y_send.at[0], y_recv.at[0], opposite)]
+    s_copies = [forward(own, sb_send.at[0], sb_recv.at[0], sibling)]
+    for dz in (1, 3, 2):
+        z_copies[dz].wait_recv()
+        got = block((z + 4 - dz) % 4, y, c)
+        y_copies.append(forward(got, y_send.at[dz], y_recv.at[dz], opposite))
+        s_copies.append(forward(got, sb_send.at[dz], sb_recv.at[dz], sibling))
+
+    for load in loads:
+        load.wait()
+
+    def inward(yy):
+        block_rows = rows[pl.ds(pl.multiple_of(yy * 64, 64), 64), :]
+        both = jnp.dot(block_rows, w_in[...], preferred_element_type=jnp.float32)
+        acc_gu[pl.ds(pl.multiple_of(yy * 32, 32), 32), :] = both.reshape(4, 16, 256)[:, 0:8].reshape(32, 256)
+
+    def back(yy):
+        block_rows = rows[pl.ds(pl.multiple_of(yy * 64, 64), 64), :]
+        out = lax.dot_general(block_rows, w_down[...], (((1,), (1,)), ((), ())), preferred_element_type=jnp.float32)
+        acc_dh[pl.ds(pl.multiple_of(yy * 32, 32), 32), :] = out.reshape(4, 16, 128)[:, 8:16].reshape(32, 128)
+
+    for copy in s_copies:
+        copy.wait_recv()
+    inward(y)
+    last = []
+    for n, dz in enumerate((0, 1, 3, 2)):
+        y_copies[n].wait_recv()
+        got = block((z + 4 - dz) % 4, 1 - y, c)
+        last.append(forward(got, sb_send.at[4 + dz], sb_recv.at[4 + dz], sibling))
+    back(y)
+    for copy in last:
+        copy.wait_recv()
+    inward(1 - y)
+    back(1 - y)
+
+    keep = jnp.where(rank_ref[0, 0] < kept_ref[0], 1.0, 0.0).astype(jnp.float32)
+    gate_pre = acc_gu[:, 0:128]
+    up_pre = acc_gu[:, 128:256]
+    hidden_grad = acc_dh[...]
+    sigmoid_gate = jax.nn.sigmoid(gate_pre)
+    activated = gate_pre * sigmoid_gate
+    hidden = activated * up_pre * keep
+    up_grad = hidden_grad * activated * keep
+    gate_grad = hidden_grad * up_pre * sigmoid_gate * (1.0 + gate_pre * (1.0 - sigmoid_gate)) * keep
+    both_grad = jnp.concatenate([gate_grad, up_grad], axis=1)
+    both_bf16 = both_grad.astype(jnp.bfloat16)
+
+    def partial(hh):
+        w_half = w_in[pl.ds(pl.multiple_of(hh * half, 256), half), :]
+        term = lax.dot_general(both_bf16, w_half, (((1,), (1,)), ((), ())), preferred_element_type=jnp.float32)
+        low = term[:, :pair].reshape(8, 8, pair)
+        high = term[:, pair:].reshape(8, 8, pair)
+        return jnp.concatenate([low, high], axis=1).reshape(128, pair)
+
+    sib_out[...] = partial(1 - c).astype(jnp.bfloat16)
+    sib_copy = remote(sib_out, sib_in, r1_send, r1_recv, sibling)
+    sib_copy.start()
+    sends.append(sib_copy)
+    part[...] = partial(c)
+
+    zeros = jnp.zeros((8, 8, 128), jnp.float32)
+    hidden_pad = jnp.concatenate([zeros, hidden.reshape(8, 8, 128)], axis=1).reshape(128, 128).astype(jnp.bfloat16)
+    zeros2 = jnp.zeros((8, 8, 256), jnp.float32)
+    both_pad = jnp.concatenate([both_grad.reshape(8, 8, 256), zeros2], axis=1).reshape(128, 256).astype(jnp.bfloat16)
+
+    sib_copy.wait_recv()
+    total = part[...] + sib_in[...].astype(jnp.float32)
+    part[...] = total
+    unit[...] = total.astype(jnp.bfloat16)
+    unit_copies = []
+    for dz, dy in sorted(chips, key=lambda p: p[0] != 2):
+        index = dz * 2 + dy
+        target = ((y + dy) % 2) * 4 + (z + dz) % 4
+        copy = remote(
+            unit.at[pl.ds(pl.multiple_of(target * 16, 16), 16), :], unit_in.at[index],
+            r2_send.at[index], r2_recv.at[index], chip_device(dz, dy),
+        )
+        copy.start()
+        sends.append(copy)
+        unit_copies.append(copy)
+
+    for n in range(4):
+        columns = pl.ds(n * pair, pair)
+        some = rows[:, columns]
+        grad_down[:, columns] = lax.dot_general(
+            hidden_pad, some, (((0,), (0,)), ((), ())), preferred_element_type=jnp.float32
+        ).astype(jnp.bfloat16)
+        grad_in[columns, :] = lax.dot_general(
+            some, both_pad, (((0,), (0,)), ((), ())), preferred_element_type=jnp.float32
+        ).astype(jnp.bfloat16)
+    stores = [
+        pltpu.make_async_copy(grad_down, down_out.at[0], store_sem.at[0]),
+        pltpu.make_async_copy(grad_in.at[:, pl.ds(0, 128)], gate_out.at[0], store_sem.at[1]),
+        pltpu.make_async_copy(grad_in.at[:, pl.ds(128, 128)], up_out.at[0], store_sem.at[2]),
+    ]
+    for store in stores:
+        store.start()
+
+    for copy in unit_copies:
+        copy.wait_recv()
+    result = part[my_rows, :]
+    for dz, dy in chips:
+        result = result + unit_in[dz * 2 + dy].astype(jnp.float32)
+    final_out[...] = result.astype(jnp.bfloat16)
+    place = pl.ds(pl.multiple_of((s * 2 + c) * 16, 16), 16)
+    finals = []
+    for de, dc in near:
+        index = de * 2 + dc
+        copy = remote(final_out, final_in.at[place, :], f_send.at[index], f_recv.at[index], near_device(de, dc))
+        copy.start()
+        finals.append(copy)
+    final_in[place, :] = final_out[...]
+    for copy in finals:
+        copy.wait_recv()
+    sends += finals
+    rows_out[...] = jnp.dot(chosen, final_in[...], preferred_element_type=jnp.float32).astype(jnp.bfloat16)
+    for copy in sends:
+        copy.wait_send()
+    for store in stores:
+        store.wait()
+
+
+def kernel_body(x_rows, cot_rows, counts, w_gate, w_up, w_down, kept_blocks, block_rank):
+    width = x_rows.shape[4]
+    quarter = width // 8
+    pair = width // 4
+
+    def cut(slots):
+        return jnp.transpose(slots.reshape(2, 2, 2, 4, quarter), (0, 2, 1, 3, 4))
+
+    prep = jnp.stack([cut(x_rows), cut(cot_rows)], axis=2).reshape(2, 2, 16, quarter)
+    vmem = pl.BlockSpec(memory_space=pltpu.VMEM)
+    smem = pl.BlockSpec(memory_space=pltpu.SMEM)
+    hbm = pl.BlockSpec(memory_space=pl.ANY)
+    bf16, f32 = jnp.bfloat16, jnp.float32
+    dma = pltpu.SemaphoreType.DMA
+    out_rows, grad_gate, grad_up, grad_down = pl.pallas_call(
+        exchange_kernel,
+        out_shape=(
+            jax.ShapeDtypeStruct((16, pair), bf16),
+            jax.ShapeDtypeStruct(w_gate.shape, bf16),
+            jax.ShapeDtypeStruct(w_up.shape, bf16),
+            jax.ShapeDtypeStruct(w_down.shape, bf16),
+        ),
+        in_specs=[vmem, smem, smem, smem, hbm, hbm, hbm],
+        out_specs=(vmem, hbm, hbm, hbm),
+        scratch_shapes=[
+            pltpu.VMEM((2, 2, 16, quarter), bf16),
+            pltpu.VMEM((64, quarter), bf16),
+            pltpu.VMEM((128, width), bf16),
+            pltpu.VMEM((width, 256), bf16),
+            pltpu.VMEM((128, width), bf16),
+            pltpu.VMEM((64, 256), f32),
+            pltpu.VMEM((64, 128), f32),
+            pltpu.VMEM((128, pair), bf16),
+            pltpu.VMEM((128, pair), bf16),
+            pltpu.VMEM((128, pair), f32),
+            pltpu.VMEM((128, pair), bf16),
+            pltpu.VMEM((8, 16, pair), bf16),
+            pltpu.VMEM((16, pair), bf16),
+            pltpu.VMEM((64, pair), bf16),
+            pltpu.VMEM((width, 256), bf16),
+            pltpu.VMEM((128, width), bf16),
+            dma((4,)), dma((4,)), dma((3,)), dma((3,)), dma((4,)), dma((4,)), dma((8,)), dma((8,)),
+            dma(()), dma(()), dma((8,)), dma((8,)), dma((4,)), dma((4,)), dma((3,)), dma((3,)),
+        ],
+        compiler_params=pltpu.CompilerParams(
+            collective_id=0, has_side_effects=True, vmem_limit_bytes=32 * 1024 * 1024
+        ),
+        name="expert_backward",
+    )(prep, counts, kept_blocks, block_rank, w_gate, w_up, w_down)
+    return (out_rows.reshape(x_rows.shape), grad_gate, grad_up, grad_down)
+
+
 def solution(mesh):
     in_specs = (
         P("expert", "dp", None, None, None),
@@ -90,4 +381,5 @@
         P("expert", None, "dp"),
         P("expert", "dp", None),
     )
-    return jax.shard_map(body, mesh=mesh, in_specs=in_specs, out_specs=out_specs, check_vma=False)
+    small = mesh.shape["expert"] == 2 and mesh.shape["dp"] == 16
+    return jax.shard_map(kernel_body if small else body, mesh=mesh, in_specs=in_specs, out_specs=out_specs, check_vma=False)

time: 138 us -> 42.8 us (0.31)
  blocking collectives: 110 us -> 0 us
  Pallas kernels: 0 us -> 32.3 us
  starting transfers between devices: 10.9 us -> 0 us
  matrix products: 8.04 us -> 0 us
  local copies, waits for them, and re-layouts: 2.89 us -> 8.14 us
  waiting for transfers between devices: 2.62 us -> 0 us
    unnamed x1 -> x0, blocking collectives: 67.7 us -> none
    all_gather x2 -> x0, blocking collectives: 41.9 us -> none  [the longest x1 23.2 us: body(): lax.all_gather(pack_rows(got_rows), 'dp', axis=0, tiled=True)]
    pallas_call x0 -> x1, Pallas kernels: none -> 32.3 us  [kernel_body(): pl.pallas_call(exchange_kernel, out_shape=(jax.ShapeDtypeStruct((16, pair...]
    all_to_all x3 -> x0, starting transfers between devices: 10.9 us -> none  [the longest x1 4.35 us: body(): lax.all_to_all(slot_rows, 'expert', split_axis=0, concat_axis=0, tiled=True)]
    dot_general x11 -> x0, matrix products: 8.04 us -> none  [the longest x7 6.01 us: contract(): lax.dot_general(left, right, (((left_dim,), (right_dim,)), ((), ())), pre...]
    unnamed x22 -> x13, local copies, waits for them, and re-layouts: 2.08 us -> 6.69 us
    all_to_all x3 -> x0, waiting for transfers between devices: 2.62 us -> none  [the longest x1 2.61 us: body(): lax.all_to_all(slot_grads, 'expert', split_axis=0, concat_axis=0, tiled=T...]
  transfers between devices with their start and end apart: 3 -> 0, of which waited for: 1 -> 0; matrix products, arithmetic and copies ran while one was open for 4% -> 0% of each run, Pallas kernels for 0% -> 0%
where the time goes in v1:
time: 42.8 us; the launch traced here: 42.5 us
  Pallas kernels  32.3 us (75%)
  local copies, waits for them, and re-layouts  8.14 us (19%)
  between operations  1.99 us (5%)
    pallas_call x1, Pallas kernels, kernel_body(): pl.pallas_call(exchange_kernel, out_shape=(jax.ShapeDtypeStruct((16, pair...  32.3 us
    unnamed x13, local copies, waits for them, and re-layouts  6.69 us

profile of v1, /device:TPU:0, one launch (start us, length us, event | category | flops | bytes accessed | tf_op | source)
XLA Modules:
  0.0 42.5 jit_solution(5767752044573219283)
XLA Ops:
  1.9 0.0 copy-start.4
  1.9 0.8 %reshape.20 = bf16[2,2,2,4,384]{4,3,2,1,0:T(4,128)(2,1)S(1)} reshape(bf16[1,1,2,2,3072]{4,3,2,1,0:T(2,128)(2,1)} %param.8) | data formatting | bytes 49152 | tf_op jit(solution)/shard_map/reshape | solution.py:321
  2.7 0.0 copy-done.4
  2.8 0.0 copy-start.3
  2.8 0.6 %copy-done.3 = s32[2,1,2]{2,1,0:T(1,128)S(1)} copy-done((s32[2,1,2]{2,1,0:T(1,128)S(1)}, s32[2,1,2]{2,1,0:T(1,128)}, u32[]{:S(2)}) %copy-start.3) | copy-done | bytes 40
  3.5 0.0 copy-start
  3.5 1.1 %copy-done = bf16[1,3072,128]{2,1,0:T(8,128)(2,1)S(1)} copy-done((bf16[1,3072,128]{2,1,0:T(8,128)(2,1)S(1)}, bf16[1,3072,128]{2,1,0:T(8,128)(2,1)}, u32[]{:S(2)}) %copy-start) | copy-done | bytes 786456
  4.6 0.0 copy-start.1
  4.6 1.1 %copy-done.1 = bf16[1,3072,128]{2,1,0:T(8,128)(2,1)S(1)} copy-done((bf16[1,3072,128]{2,1,0:T(8,128)(2,1)S(1)}, bf16[1,3072,128]{2,1,0:T(8,128)(2,1)}, u32[]{:S(2)}) %copy-start.1) | copy-done | bytes 786456
  5.8 0.0 copy-start.2
  5.8 1.1 %copy-done.2 = bf16[1,128,3072]{2,1,0:T(8,128)(2,1)S(1)} copy-done((bf16[1,128,3072]{2,1,0:T(8,128)(2,1)S(1)}, bf16[1,128,3072]{2,1,0:T(8,128)(2,1)}, u32[]{:S(2)}) %copy-start.2) | copy-done | bytes 786456
  6.9 32.3 %expert_backward.1 = (bf16[16,768]{1,0:T(8,128)(2,1)S(1)}, bf16[1,3072,128]{2,1,0:T(8,128)(2,1)S(1)}, bf16[1,3072,128]{2,1,0:T(8,128)(2,1)S(1)}, bf16[1,128,3072]{2,1,0:T(8,128)(2,1)S(1)}) custom-call(bf16[2,2,16,384]{3,2,1,0:T(8,128)(2,1)S(1)} %reshape.22.prep_ref, s32[2,1,2]{2,1,0:T(1,128)S(1)} %copy-done.3, s32[1]{0:T(128)S(6)} %copy.19.kept_ref, ...), custom_call_target="tpu_custom_call" | custom-call | tf_op jit(solution)/shard_map/expert_backward/pallas_call | solution.py:329
  39.2 0.6 %reshape.23 = bf16[1,1,2,2,3072]{4,3,2,1,0:T(2,128)(2,1)} reshape(bf16[16,768]{1,0:T(8,128)(2,1)S(1)} %get-tuple-element.8) | data formatting | bytes 49152 | tf_op jit(solution)/shard_map/reshape | solution.py:364
  39.8 0.9 %copy.21 = bf16[1,3072,128]{2,1,0:T(8,128)(2,1)} copy(bf16[1,3072,128]{2,1,0:T(8,128)(2,1)S(1)} %get-tuple-element.19) | data formatting | bytes 1572864
  40.7 0.9 %copy.22 = bf16[1,3072,128]{2,1,0:T(8,128)(2,1)} copy(bf16[1,3072,128]{2,1,0:T(8,128)(2,1)S(1)} %get-tuple-element.20) | data formatting | bytes 1572864
  41.6 0.9 %copy.23 = bf16[1,128,3072]{2,1,0:T(8,128)(2,1)} copy(bf16[1,128,3072]{2,1,0:T(8,128)(2,1)S(1)} %get-tuple-element.21) | data formatting | bytes 1572864
  (4 shorter events, 0.1 us)
Async XLA Ops:
  1.9 0.8 %copy-start.4 = (bf16[1,1,2,2,3072]{4,3,2,1,0:T(2,128)(2,1)S(1)}, bf16[1,1,2,2,3072]{4,3,2,1,0:T(2,128)(2,1)}, u32[]{:S(2)}) copy-start(bf16[1,1,2,2,3072]{4,3,2,1,0:T(2,128)(2,1)} %param.9) | copy-start | bytes 73732
  2.8 0.7 %copy-start.3 = (s32[2,1,2]{2,1,0:T(1,128)S(1)}, s32[2,1,2]{2,1,0:T(1,128)}, u32[]{:S(2)}) copy-start(s32[2,1,2]{2,1,0:T(1,128)} %counts_ref.1) | copy-start | bytes 52
  3.5 1.1 %copy-start = (bf16[1,3072,128]{2,1,0:T(8,128)(2,1)S(1)}, bf16[1,3072,128]{2,1,0:T(8,128)(2,1)}, u32[]{:S(2)}) copy-start(bf16[1,3072,128]{2,1,0:T(8,128)(2,1)} %wg_ref.1) | copy-start | bytes 2359300
  4.6 1.1 %copy-start.1 = (bf16[1,3072,128]{2,1,0:T(8,128)(2,1)S(1)}, bf16[1,3072,128]{2,1,0:T(8,128)(2,1)}, u32[]{:S(2)}) copy-start(bf16[1,3072,128]{2,1,0:T(8,128)(2,1)} %wu_ref.1) | copy-start | bytes 2359300
  5.8 1.1 %copy-start.2 = (bf16[1,128,3072]{2,1,0:T(8,128)(2,1)S(1)}, bf16[1,128,3072]{2,1,0:T(8,128)(2,1)}, u32[]{:S(2)}) copy-start(bf16[1,128,3072]{2,1,0:T(8,128)(2,1)} %wd_ref.1) | copy-start | bytes 2359300

commit v2 on v1

--- a/solution.py
+++ b/solution.py
@@ -76,12 +76,12 @@
 
 
 def exchange_kernel(
-    prep_ref, counts_ref, kept_ref, rank_ref, wg_ref, wu_ref, wd_ref,
-    rows_out, gate_out, up_out, down_out,
-    stage, landed, rows, w_in, w_down, acc_gu, acc_dh, sib_out, sib_in, part, unit, unit_in,
-    final_out, final_in, grad_in, grad_down,
+    x_ref, cot_ref, counts_hbm, kept_ref, rank_ref, wg_ref, wu_ref, wd_ref,
+    final_in, gate_out, up_out, down_out,
+    slots, counts_ref,
+    stage, landed, rows, w_in, w_down, acc_gu, acc_dh, sib_out, sib_in, part, unit, unit_in, final_out,
     s1_send, s1_recv, z_send, z_recv, y_send, y_recv, sb_send, sb_recv,
-    r1_send, r1_recv, r2_send, r2_recv, f_send, f_recv, load_sem, store_sem,
+    r1_send, r1_recv, r2_send, r2_recv, f_send, f_recv, load_sem, slot_sem,
 ):
     s = lax.axis_index("expert")
     d = lax.axis_index("dp")
@@ -109,6 +109,11 @@
     def chip_device(dz, dy):
         return device(s, (z + dz) % 4, (y + dy) % 2, c)
 
+    slot_loads = [
+        pltpu.make_async_copy(x_ref.at[0, 0], slots.at[0], slot_sem.at[0]),
+        pltpu.make_async_copy(cot_ref.at[0, 0], slots.at[1], slot_sem.at[1]),
+        pltpu.make_async_copy(counts_hbm, counts_ref, slot_sem.at[2]),
+    ]
     loads = [
         pltpu.make_async_copy(wg_ref.at[0], w_in.at[:, pl.ds(0, 128)], load_sem.at[0]),
         pltpu.make_async_copy(wu_ref.at[0], w_in.at[:, pl.ds(128, 128)], load_sem.at[1]),
@@ -119,15 +124,23 @@
         pl.semaphore_signal(barrier, inc=1, device_id=near_device(de, dc), device_id_type=pl.DeviceIdType.MESH)
     for dz, dy in chips:
         pl.semaphore_signal(barrier, inc=1, device_id=chip_device(dz, dy), device_id_type=pl.DeviceIdType.MESH)
-    for load in loads:
+    for load in slot_loads + loads:
         load.start()
+    for load in slot_loads:
+        load.wait()
 
     row16 = lax.broadcasted_iota(jnp.int32, (16, quarter), 0)
     slot = (row16 >> 2) & 1
     for e in range(2):
         live = jnp.where(s == 0, counts_ref[0, 0, e], counts_ref[1, 0, e])
+        sources = [slots[0, e].astype(jnp.float32), slots[1, e].astype(jnp.float32)]
         for h in range(2):
-            value = prep_ref[e, h].astype(jnp.float32)
+            value = jnp.zeros((16, quarter), jnp.float32)
+            for r in range(16):
+                t, k, g = r // 8, (r // 4) % 2, r % 4
+                start = h * half + g * quarter
+                line = sources[t][k:k + 1, start:start + quarter]
+                value = jnp.where(row16 == r, jnp.broadcast_to(line, value.shape), value)
             stage[e, h] = jnp.where(slot < live, value, 0.0).astype(jnp.bfloat16)
 
     i = lax.broadcasted_iota(jnp.int32, (64, 64), 0)
@@ -138,16 +151,6 @@
         & (((i >> 2) & 1) == ((j >> 5) & 1))
         & (((i >> 1) & 1) == ((j >> 4) & 1))
         & ((i & 1) == ((j >> 2) & 1))
-    ).astype(jnp.float32).astype(jnp.bfloat16)
-    oi = lax.broadcasted_iota(jnp.int32, (16, 64), 0)
-    oj = lax.broadcasted_iota(jnp.int32, (16, 64), 1)
-    chosen = (
-        ((oi >> 3) == (oj >> 5))
-        & (((oi >> 2) & 1) == (oj & 1))
-        & (((oi >> 1) & 1) == ((oj >> 4) & 1))
-        & ((oi & 1) == ((oj >> 3) & 1))
-        & (((oj >> 2) & 1) == c)
-        & (((oj >> 1) & 1) == s)
     ).astype(jnp.float32).astype(jnp.bfloat16)
 
     pl.semaphore_wait(barrier, len(near) + len(chips))
@@ -201,29 +204,40 @@
     for load in loads:
         load.wait()
 
-    def inward(yy):
-        block_rows = rows[pl.ds(pl.multiple_of(yy * 64, 64), 64), :]
-        both = jnp.dot(block_rows, w_in[...], preferred_element_type=jnp.float32)
-        acc_gu[pl.ds(pl.multiple_of(yy * 32, 32), 32), :] = both.reshape(4, 16, 256)[:, 0:8].reshape(32, 256)
-
-    def back(yy):
-        block_rows = rows[pl.ds(pl.multiple_of(yy * 64, 64), 64), :]
-        out = lax.dot_general(block_rows, w_down[...], (((1,), (1,)), ((), ())), preferred_element_type=jnp.float32)
-        acc_dh[pl.ds(pl.multiple_of(yy * 32, 32), 32), :] = out.reshape(4, 16, 128)[:, 8:16].reshape(32, 128)
-
-    for copy in s_copies:
-        copy.wait_recv()
-    inward(y)
+    def forward_part(yy, hh, start):
+        columns = pl.ds(pl.multiple_of(hh * half, 256), half)
+        some = rows[pl.ds(pl.multiple_of(yy * 64, 64), 64), columns]
+        both = jnp.dot(some, w_in[columns, :], preferred_element_type=jnp.float32)
+        back = lax.dot_general(
+            some, w_down[:, columns], (((1,), (1,)), ((), ())), preferred_element_type=jnp.float32
+        )
+        both = both.reshape(4, 16, 256)[:, 0:8].reshape(32, 256)
+        back = back.reshape(4, 16, 128)[:, 8:16].reshape(32, 128)
+        place = pl.ds(pl.multiple_of(yy * 32, 32), 32)
+        if not start:
+            both = both + acc_gu[place, :]
+            back = back + acc_dh[place, :]
+        acc_gu[place, :] = both
+        acc_dh[place, :] = back
+
     last = []
-    for n, dz in enumerate((0, 1, 3, 2)):
+
+    def pass_on(n, dz):
         y_copies[n].wait_recv()
         got = block((z + 4 - dz) % 4, 1 - y, c)
         last.append(forward(got, sb_send.at[4 + dz], sb_recv.at[4 + dz], sibling))
-    back(y)
+
+    forward_part(y, c, True)
+    pass_on(0, 0)
+    for copy in s_copies:
+        copy.wait_recv()
+    forward_part(y, 1 - c, False)
+    for n, dz in ((1, 1), (2, 3), (3, 2)):
+        pass_on(n, dz)
+    forward_part(1 - y, c, True)
     for copy in last:
         copy.wait_recv()
-    inward(1 - y)
-    back(1 - y)
+    forward_part(1 - y, 1 - c, False)
 
     keep = jnp.where(rank_ref[0, 0] < kept_ref[0], 1.0, 0.0).astype(jnp.float32)
     gate_pre = acc_gu[:, 0:128]
@@ -274,19 +288,14 @@
     for n in range(4):
         columns = pl.ds(n * pair, pair)
         some = rows[:, columns]
-        grad_down[:, columns] = lax.dot_general(
+        down_out[0, :, columns] = lax.dot_general(
             hidden_pad, some, (((0,), (0,)), ((), ())), preferred_element_type=jnp.float32
         ).astype(jnp.bfloat16)
-        grad_in[columns, :] = lax.dot_general(
+        inner = lax.dot_general(
             some, both_pad, (((0,), (0,)), ((), ())), preferred_element_type=jnp.float32
         ).astype(jnp.bfloat16)
-    stores = [
-        pltpu.make_async_copy(grad_down, down_out.at[0], store_sem.at[0]),
-        pltpu.make_async_copy(grad_in.at[:, pl.ds(0, 128)], gate_out.at[0], store_sem.at[1]),
-        pltpu.make_async_copy(grad_in.at[:, pl.ds(128, 128)], up_out.at[0], store_sem.at[2]),
-    ]
-    for store in stores:
-        store.start()
+        gate_out[0, columns, :] = inner[:, 0:128]
+        up_out[0, columns, :] = inner[:, 128:256]
 
     for copy in unit_copies:
         copy.wait_recv()
@@ -305,11 +314,38 @@
     for copy in finals:
         copy.wait_recv()
     sends += finals
-    rows_out[...] = jnp.dot(chosen, final_in[...], preferred_element_type=jnp.float32).astype(jnp.bfloat16)
     for copy in sends:
         copy.wait_send()
-    for store in stores:
-        store.wait()
+
+
+def finish_kernel(final_ref, gate_ref, up_ref, down_ref, rows_out, gate_out, up_out, down_out, sem):
+    copies = [
+        pltpu.make_async_copy(gate_ref, gate_out, sem.at[0]),
+        pltpu.make_async_copy(up_ref, up_out, sem.at[1]),
+        pltpu.make_async_copy(down_ref, down_out, sem.at[2]),
+    ]
+    for copy in copies:
+        copy.start()
+    s = lax.axis_index("expert")
+    c = lax.axis_index("dp") % 2
+    pair = final_ref.shape[1]
+    i = lax.broadcasted_iota(jnp.int32, (16, 64), 0)
+    j = lax.broadcasted_iota(jnp.int32, (16, 64), 1)
+    chosen = (
+        ((i >> 3) == (j >> 5))
+        & (((i >> 2) & 1) == ((j >> 4) & 1))
+        & (((i >> 1) & 1) == ((j >> 3) & 1))
+        & ((i & 1) == (j & 1))
+        & (((j >> 2) & 1) == c)
+        & (((j >> 1) & 1) == s)
+    ).astype(jnp.float32).astype(jnp.bfloat16)
+    picked = jnp.dot(chosen, final_ref[...], preferred_element_type=jnp.float32)
+    for e in range(2):
+        for g in range(4):
+            start = e * 8 + g * 2
+            rows_out[0, 0, e, :, g * pair:(g + 1) * pair] = picked[start:start + 2, :].astype(jnp.bfloat16)
+    for copy in copies:
+        copy.wait()
 
 
 def kernel_body(x_rows, cot_rows, counts, w_gate, w_up, w_down, kept_blocks, block_rank):
@@ -317,26 +353,28 @@
     quarter = width // 8
     pair = width // 4
 
-    def cut(slots):
-        return jnp.transpose(slots.reshape(2, 2, 2, 4, quarter), (0, 2, 1, 3, 4))
-
-    prep = jnp.stack([cut(x_rows), cut(cot_rows)], axis=2).reshape(2, 2, 16, quarter)
     vmem = pl.BlockSpec(memory_space=pltpu.VMEM)
+    hbm = pl.BlockSpec(memory_space=pltpu.HBM)
+    anywhere = pl.BlockSpec(memory_space=pl.ANY)
     smem = pl.BlockSpec(memory_space=pltpu.SMEM)
-    hbm = pl.BlockSpec(memory_space=pl.ANY)
+    held = [
+        pltpu.with_memory_space_constraint(a, pltpu.HBM) for a in (x_rows, cot_rows, counts, w_gate, w_up, w_down)
+    ]
     bf16, f32 = jnp.bfloat16, jnp.float32
     dma = pltpu.SemaphoreType.DMA
-    out_rows, grad_gate, grad_up, grad_down = pl.pallas_call(
+    final_rows, grad_gate, grad_up, grad_down = pl.pallas_call(
         exchange_kernel,
         out_shape=(
-            jax.ShapeDtypeStruct((16, pair), bf16),
+            jax.ShapeDtypeStruct((64, pair), bf16),
             jax.ShapeDtypeStruct(w_gate.shape, bf16),
             jax.ShapeDtypeStruct(w_up.shape, bf16),
             jax.ShapeDtypeStruct(w_down.shape, bf16),
         ),
-        in_specs=[vmem, smem, smem, smem, hbm, hbm, hbm],
-        out_specs=(vmem, hbm, hbm, hbm),
+        in_specs=[hbm, hbm, hbm, smem, smem, hbm, hbm, hbm],
+        out_specs=(vmem, vmem, vmem, vmem),
         scratch_shapes=[
+            pltpu.VMEM((2,) + x_rows.shape[2:], bf16),
+            pltpu.SMEM(counts.shape, jnp.int32),
             pltpu.VMEM((2, 2, 16, quarter), bf16),
             pltpu.VMEM((64, quarter), bf16),
             pltpu.VMEM((128, width), bf16),
@@ -350,9 +388,6 @@
             pltpu.VMEM((128, pair), bf16),
             pltpu.VMEM((8, 16, pair), bf16),
             pltpu.VMEM((16, pair), bf16),
-            pltpu.VMEM((64, pair), bf16),
-            pltpu.VMEM((width, 256), bf16),
-            pltpu.VMEM((128, width), bf16),
             dma((4,)), dma((4,)), dma((3,)), dma((3,)), dma((4,)), dma((4,)), dma((8,)), dma((8,)),
             dma(()), dma(()), dma((8,)), dma((8,)), dma((4,)), dma((4,)), dma((3,)), dma((3,)),
         ],
@@ -360,8 +395,16 @@
             collective_id=0, has_side_effects=True, vmem_limit_bytes=32 * 1024 * 1024
         ),
         name="expert_backward",
-    )(prep, counts, kept_blocks, block_rank, w_gate, w_up, w_down)
-    return (out_rows.reshape(x_rows.shape), grad_gate, grad_up, grad_down)
+    )(*held[:3], kept_blocks, block_rank, *held[3:])
+    return pl.pallas_call(
+        finish_kernel,
+        out_shape=tuple(jax.ShapeDtypeStruct(a.shape, bf16) for a in (x_rows, w_gate, w_up, w_down)),
+        in_specs=[vmem, anywhere, anywhere, anywhere],
+        out_specs=(vmem, anywhere, anywhere, anywhere),
+        scratch_shapes=[dma((3,))],
+        compiler_params=pltpu.CompilerParams(vmem_limit_bytes=16 * 1024 * 1024),
+        name="write_outputs",
+    )(final_rows, grad_gate, grad_up, grad_down)
 
 
 def solution(mesh):

time: 42.8 us -> 35.4 us (0.83)
  local copies, waits for them, and re-layouts: 8.14 us -> 0 us
  Pallas kernels: 32.3 us -> 33.3 us
    unnamed x13 -> x0, local copies, waits for them, and re-layouts: 6.69 us -> none
    reshape x4 -> x0, local copies, waits for them, and re-layouts: 1.43 us -> none  [the longest x2 0.79 us: cut(): return jnp.transpose(slots.reshape(2, 2, 2, 4, quarter), (0, 2, 1, 3, 4))]
    pallas_call x1 -> x2, Pallas kernels: 32.3 us -> 33.3 us  [the longest x1 31.2 us: kernel_body(): pl.pallas_call(exchange_kernel, out_shape=(jax.ShapeDtypeStruct((64, pair...]
where the time goes in v2:
time: 35.4 us; the launch traced here: 35.2 us
  Pallas kernels  33.3 us (94%)
  between operations  1.93 us (5%)
    pallas_call x1, Pallas kernels, kernel_body(): pl.pallas_call(exchange_kernel, out_shape=(jax.ShapeDtypeStruct((64, pair...  31.2 us
    pallas_call x1, Pallas kernels, kernel_body(): pl.pallas_call(finish_kernel, out_shape=tuple((jax.ShapeDtypeStruct(a.sha...  2.04 us

profile of v2, /device:TPU:0, one launch (start us, length us, event | category | flops | bytes accessed | tf_op | source)
XLA Modules:
  0.0 35.2 jit_solution(5546129764310584964)
XLA Ops:
  1.9 31.2 %expert_backward.1 = (bf16[64,768]{1,0:T(8,128)(2,1)S(1)}, bf16[1,3072,128]{2,1,0:T(8,128)(2,1)S(1)}, bf16[1,3072,128]{2,1,0:T(8,128)(2,1)S(1)}, bf16[1,128,3072]{2,1,0:T(8,128)(2,1)S(1)}) custom-call(bf16[1,1,2,2,3072]{4,3,2,1,0:T(2,128)(2,1)} %x_ref.1, bf16[1,1,2,2,3072]{4,3,2,1,0:T(2,128)(2,1)} %cot_ref.1, s32[2,1,2]{2,1,0:T(1,128)} %counts_hbm.1, ...), custom_call_target="tpu_custom_call" | custom-call | tf_op jit(solution)/shard_map/expert_backward/pallas_call | solution.py:365
  33.1 2.0 %write_outputs.1 = (bf16[1,1,2,2,3072]{4,3,2,1,0:T(2,128)(2,1)}, bf16[1,3072,128]{2,1,0:T(8,128)(2,1)}, bf16[1,3072,128]{2,1,0:T(8,128)(2,1)}, bf16[1,128,3072]{2,1,0:T(8,128)(2,1)}) custom-call(bf16[64,768]{1,0:T(8,128)(2,1)S(1)} %get-tuple-element.8.final_ref, bf16[1,3072,128]{2,1,0:T(8,128)(2,1)S(1)} %get-tuple-element.9.gate_ref, ...), custom_call_target="tpu_custom_call" | custom-call | tf_op jit(solution)/shard_map/write_outputs/pallas_call | solution.py:399

commit v3 on v2

--- a/solution.py
+++ b/solution.py
@@ -77,11 +77,11 @@
 
 def exchange_kernel(
     x_ref, cot_ref, counts_hbm, kept_ref, rank_ref, wg_ref, wu_ref, wd_ref,
-    final_in, gate_out, up_out, down_out,
+    final_out, gate_out, up_out, down_out,
     slots, counts_ref,
-    stage, landed, rows, w_in, w_down, acc_gu, acc_dh, sib_out, sib_in, part, unit, unit_in, final_out,
+    stage, landed, rows, w_in, w_down, acc_gu, acc_dh, sib_out, sib_in, part, regroup, unit, unit_in,
     s1_send, s1_recv, z_send, z_recv, y_send, y_recv, sb_send, sb_recv,
-    r1_send, r1_recv, r2_send, r2_recv, f_send, f_recv, load_sem, slot_sem,
+    r1_send, r1_recv, r2_send, r2_recv, load_sem, slot_sem,
 ):
     s = lax.axis_index("expert")
     d = lax.axis_index("dp")
@@ -101,13 +101,13 @@
         )
 
     near = [(0, 1), (1, 0), (1, 1)]
-    chips = [(dz, dy) for dz in range(4) for dy in range(2) if (dz, dy) != (0, 0)]
+    others = [(de, dz, dy) for dz in (2, 3, 1, 0) for de in (1, 0) for dy in (1, 0) if (de, dz, dy) != (0, 0, 0)]
 
     def near_device(de, dc):
         return device((s + de) % 2, z, y, (c + dc) % 2)
 
-    def chip_device(dz, dy):
-        return device(s, (z + dz) % 4, (y + dy) % 2, c)
+    def other_device(de, dz, dy):
+        return device((s + de) % 2, (z + dz) % 4, (y + dy) % 2, c)
 
     slot_loads = [
         pltpu.make_async_copy(x_ref.at[0, 0], slots.at[0], slot_sem.at[0]),
@@ -120,10 +120,9 @@
         pltpu.make_async_copy(wd_ref.at[0], w_down, load_sem.at[2]),
     ]
     barrier = pltpu.get_barrier_semaphore()
-    for de, dc in near:
-        pl.semaphore_signal(barrier, inc=1, device_id=near_device(de, dc), device_id_type=pl.DeviceIdType.MESH)
-    for dz, dy in chips:
-        pl.semaphore_signal(barrier, inc=1, device_id=chip_device(dz, dy), device_id_type=pl.DeviceIdType.MESH)
+    greeted = [near_device(0, 1), near_device(1, 1)] + [other_device(*other) for other in others]
+    for where in greeted:
+        pl.semaphore_signal(barrier, inc=1, device_id=where, device_id_type=pl.DeviceIdType.MESH)
     for load in slot_loads + loads:
         load.start()
     for load in slot_loads:
@@ -153,7 +152,7 @@
         & ((i & 1) == ((j >> 2) & 1))
     ).astype(jnp.float32).astype(jnp.bfloat16)
 
-    pl.semaphore_wait(barrier, len(near) + len(chips))
+    pl.semaphore_wait(barrier, len(greeted))
 
     mine = pl.ds(pl.multiple_of((c * 2 + s) * 16, 16), 16)
     sends = []
@@ -251,39 +250,59 @@
     both_grad = jnp.concatenate([gate_grad, up_grad], axis=1)
     both_bf16 = both_grad.astype(jnp.bfloat16)
 
-    def partial(hh):
-        w_half = w_in[pl.ds(pl.multiple_of(hh * half, 256), half), :]
-        term = lax.dot_general(both_bf16, w_half, (((1,), (1,)), ((), ())), preferred_element_type=jnp.float32)
-        low = term[:, :pair].reshape(8, 8, pair)
-        high = term[:, pair:].reshape(8, 8, pair)
-        return jnp.concatenate([low, high], axis=1).reshape(128, pair)
-
-    sib_out[...] = partial(1 - c).astype(jnp.bfloat16)
-    sib_copy = remote(sib_out, sib_in, r1_send, r1_recv, sibling)
-    sib_copy.start()
-    sends.append(sib_copy)
-    part[...] = partial(c)
+    si = lax.broadcasted_iota(jnp.int32, (64, 64), 0)
+    sj = lax.broadcasted_iota(jnp.int32, (64, 64), 1)
+    split = (
+        ((sj >> 3) == ((si & 31) >> 2))
+        & ((sj & 3) == (si & 3))
+        & (((sj >> 2) & 1) == jnp.where(si >= 32, c, 1 - c))
+    ).astype(jnp.float32).astype(jnp.bfloat16)
+    by_core = jnp.dot(split, both_bf16, preferred_element_type=jnp.float32).astype(jnp.bfloat16)
+    sib_copies = []
+    for n in range(4):
+        term = lax.dot_general(
+            by_core, w_in[n * pair:(n + 1) * pair, :], (((1,), (1,)), ((), ())), preferred_element_type=jnp.float32
+        )
+        sib_out[n] = term[0:32].astype(jnp.bfloat16)
+        copy = remote(sib_out.at[n], sib_in.at[n], r1_send.at[n], r1_recv.at[n], sibling)
+        copy.start()
+        sib_copies.append(copy)
+        part[n] = term[32:64]
+    sends += sib_copies
 
     zeros = jnp.zeros((8, 8, 128), jnp.float32)
     hidden_pad = jnp.concatenate([zeros, hidden.reshape(8, 8, 128)], axis=1).reshape(128, 128).astype(jnp.bfloat16)
     zeros2 = jnp.zeros((8, 8, 256), jnp.float32)
     both_pad = jnp.concatenate([both_grad.reshape(8, 8, 256), zeros2], axis=1).reshape(128, 256).astype(jnp.bfloat16)
 
-    sib_copy.wait_recv()
-    total = part[...] + sib_in[...].astype(jnp.float32)
-    part[...] = total
-    unit[...] = total.astype(jnp.bfloat16)
+    ui = lax.broadcasted_iota(jnp.int32, (256, 256), 0)
+    uj = lax.broadcasted_iota(jnp.int32, (256, 256), 1)
+    spread = (
+        ((uj >> 5) == ((ui >> 1) & 7))
+        & ((uj & 1) == (ui & 1))
+        & (((uj >> 1) & 1) == ((ui >> 4) & 1))
+        & (((uj >> 2) & 7) == (ui >> 5))
+    ).astype(jnp.float32).astype(jnp.bfloat16)
+    for n in range(4):
+        sib_copies[n].wait_recv()
+        total = (part[n] + sib_in[n].astype(jnp.float32)).astype(jnp.bfloat16)
+        regroup[n * 64:n * 64 + 32, :] = total[:, 0:quarter]
+        regroup[n * 64 + 32:n * 64 + 64, :] = total[:, quarter:]
+    unit[...] = jnp.dot(spread, regroup[...], preferred_element_type=jnp.float32).astype(jnp.bfloat16)
+
+    def unit_of(ee, zz, yy):
+        return unit.at[pl.ds(pl.multiple_of(((yy * 4 + zz) * 2 + ee) * 16, 16), 16), :]
+
     unit_copies = []
-    for dz, dy in sorted(chips, key=lambda p: p[0] != 2):
-        index = dz * 2 + dy
-        target = ((y + dy) % 2) * 4 + (z + dz) % 4
+    for de, dz, dy in others:
+        index = de * 8 + dz * 2 + dy
         copy = remote(
-            unit.at[pl.ds(pl.multiple_of(target * 16, 16), 16), :], unit_in.at[index],
-            r2_send.at[index], r2_recv.at[index], chip_device(dz, dy),
+            unit_of((s + de) % 2, (z + dz) % 4, (y + dy) % 2), unit_in.at[index],
+            r2_send.at[index], r2_recv.at[index], other_device(de, dz, dy),
         )
         copy.start()
-        sends.append(copy)
         unit_copies.append(copy)
+    sends += unit_copies
 
     for n in range(4):
         columns = pl.ds(n * pair, pair)
@@ -299,53 +318,43 @@
 
     for copy in unit_copies:
         copy.wait_recv()
-    result = part[my_rows, :]
-    for dz, dy in chips:
-        result = result + unit_in[dz * 2 + dy].astype(jnp.float32)
-    final_out[...] = result.astype(jnp.bfloat16)
-    place = pl.ds(pl.multiple_of((s * 2 + c) * 16, 16), 16)
-    finals = []
-    for de, dc in near:
-        index = de * 2 + dc
-        copy = remote(final_out, final_in.at[place, :], f_send.at[index], f_recv.at[index], near_device(de, dc))
-        copy.start()
-        finals.append(copy)
-    final_in[place, :] = final_out[...]
-    for copy in finals:
-        copy.wait_recv()
-    sends += finals
+    for de in range(2):
+        if de == 0:
+            result = unit[pl.ds(pl.multiple_of(((y * 4 + z) * 2 + s) * 16, 16), 16), :].astype(jnp.float32)
+        else:
+            result = unit_in[8].astype(jnp.float32)
+        for index in range(1, 8):
+            result = result + unit_in[de * 8 + index].astype(jnp.float32)
+        final_out[pl.ds(pl.multiple_of(((s + de) % 2) * 16, 16), 16), :] = result.astype(jnp.bfloat16)
     for copy in sends:
         copy.wait_send()
 
 
-def finish_kernel(final_ref, gate_ref, up_ref, down_ref, rows_out, gate_out, up_out, down_out, sem):
-    copies = [
-        pltpu.make_async_copy(gate_ref, gate_out, sem.at[0]),
-        pltpu.make_async_copy(up_ref, up_out, sem.at[1]),
-        pltpu.make_async_copy(down_ref, down_out, sem.at[2]),
-    ]
+def finish_kernel(final_ref, gate_ref, up_ref, down_ref, rows_out, gate_out, up_out, down_out, lines, sem, line_sem):
+    copies = []
+    depth = gate_ref.shape[1] // 4
+    lanes = down_ref.shape[1] // 4
+    for n in range(4):
+        some = pl.ds(n * depth, depth)
+        few = pl.ds(n * lanes, lanes)
+        copies += [
+            pltpu.make_async_copy(gate_ref.at[:, some, :], gate_out.at[:, some, :], sem.at[n]),
+            pltpu.make_async_copy(up_ref.at[:, some, :], up_out.at[:, some, :], sem.at[4 + n]),
+            pltpu.make_async_copy(down_ref.at[:, few, :], down_out.at[:, few, :], sem.at[8 + n]),
+        ]
     for copy in copies:
         copy.start()
-    s = lax.axis_index("expert")
-    c = lax.axis_index("dp") % 2
-    pair = final_ref.shape[1]
-    i = lax.broadcasted_iota(jnp.int32, (16, 64), 0)
-    j = lax.broadcasted_iota(jnp.int32, (16, 64), 1)
-    chosen = (
-        ((i >> 3) == (j >> 5))
-        & (((i >> 2) & 1) == ((j >> 4) & 1))
-        & (((i >> 1) & 1) == ((j >> 3) & 1))
-        & ((i & 1) == (j & 1))
-        & (((j >> 2) & 1) == c)
-        & (((j >> 1) & 1) == s)
-    ).astype(jnp.float32).astype(jnp.bfloat16)
-    picked = jnp.dot(chosen, final_ref[...], preferred_element_type=jnp.float32)
+    quarter = final_ref.shape[1]
+    final = final_ref[...].astype(jnp.float32)
     for e in range(2):
-        for g in range(4):
-            start = e * 8 + g * 2
-            rows_out[0, 0, e, :, g * pair:(g + 1) * pair] = picked[start:start + 2, :].astype(jnp.bfloat16)
+        for g in range(8):
+            start = e * 16 + g * 2
+            lines[0, 0, e, :, g * quarter:(g + 1) * quarter] = final[start:start + 2, :].astype(jnp.bfloat16)
+    line_copy = pltpu.make_async_copy(lines, rows_out, line_sem)
+    line_copy.start()
     for copy in copies:
         copy.wait()
+    line_copy.wait()
 
 
 def kernel_body(x_rows, cot_rows, counts, w_gate, w_up, w_down, kept_blocks, block_rank):
@@ -365,7 +374,7 @@
     final_rows, grad_gate, grad_up, grad_down = pl.pallas_call(
         exchange_kernel,
         out_shape=(
-            jax.ShapeDtypeStruct((64, pair), bf16),
+            jax.ShapeDtypeStruct((32, quarter), bf16),
             jax.ShapeDtypeStruct(w_gate.shape, bf16),
             jax.ShapeDtypeStruct(w_up.shape, bf16),
             jax.ShapeDtypeStruct(w_down.shape, bf16),
@@ -382,14 +391,14 @@
             pltpu.VMEM((128, width), bf16),
             pltpu.VMEM((64, 256), f32),
             pltpu.VMEM((64, 128), f32),
-            pltpu.VMEM((128, pair), bf16),
-            pltpu.VMEM((128, pair), bf16),
-            pltpu.VMEM((128, pair), f32),
-            pltpu.VMEM((128, pair), bf16),
-            pltpu.VMEM((8, 16, pair), bf16),
-            pltpu.VMEM((16, pair), bf16),
+            pltpu.VMEM((4, 32, pair), bf16),
+            pltpu.VMEM((4, 32, pair), bf16),
+            pltpu.VMEM((4, 32, pair), f32),
+            pltpu.VMEM((256, quarter), bf16),
+            pltpu.VMEM((256, quarter), bf16),
+            pltpu.VMEM((16, 16, quarter), bf16),
             dma((4,)), dma((4,)), dma((3,)), dma((3,)), dma((4,)), dma((4,)), dma((8,)), dma((8,)),
-            dma(()), dma(()), dma((8,)), dma((8,)), dma((4,)), dma((4,)), dma((3,)), dma((3,)),
+            dma((4,)), dma((4,)), dma((16,)), dma((16,)), dma((3,)), dma((3,)),
         ],
         compiler_params=pltpu.CompilerParams(
             collective_id=0, has_side_effects=True, vmem_limit_bytes=32 * 1024 * 1024
@@ -400,8 +409,8 @@
         finish_kernel,
         out_shape=tuple(jax.ShapeDtypeStruct(a.shape, bf16) for a in (x_rows, w_gate, w_up, w_down)),
         in_specs=[vmem, anywhere, anywhere, anywhere],
-        out_specs=(vmem, anywhere, anywhere, anywhere),
-        scratch_shapes=[dma((3,))],
+        out_specs=(anywhere, anywhere, anywhere, anywhere),
+        scratch_shapes=[pltpu.VMEM(x_rows.shape, bf16), dma((12,)), dma(())],
         compiler_params=pltpu.CompilerParams(vmem_limit_bytes=16 * 1024 * 1024),
         name="write_outputs",
     )(final_rows, grad_gate, grad_up, grad_down)

time: 35.4 us -> 34 us (0.960)
  Pallas kernels: 33.3 us -> 31.9 us
    pallas_call x1, Pallas kernels: 31.2 us -> 30.4 us  [kernel_body(): pl.pallas_call(exchange_kernel, out_shape=(jax.ShapeDtypeStruct((32, quar...]
    pallas_call x1, Pallas kernels: 2.04 us -> 1.5 us  [kernel_body(): pl.pallas_call(finish_kernel, out_shape=tuple((jax.ShapeDtypeStruct(a.sha...]
where the time goes in v3:
time: 34 us; the launch traced here: 33.8 us
  Pallas kernels  31.9 us (94%)
  between operations  1.93 us (6%)
    pallas_call x1, Pallas kernels, kernel_body(): pl.pallas_call(exchange_kernel, out_shape=(jax.ShapeDtypeStruct((32, quar...  30.4 us
    pallas_call x1, Pallas kernels, kernel_body(): pl.pallas_call(finish_kernel, out_shape=tuple((jax.ShapeDtypeStruct(a.sha...  1.5 us

profile of v3, /device:TPU:0, one launch (start us, length us, event | category | flops | bytes accessed | tf_op | source)
XLA Modules:
  0.0 33.8 jit_solution(3085494853181931473)
XLA Ops:
  1.9 30.4 %expert_backward.1 = (bf16[32,384]{1,0:T(8,128)(2,1)S(1)}, bf16[1,3072,128]{2,1,0:T(8,128)(2,1)S(1)}, bf16[1,3072,128]{2,1,0:T(8,128)(2,1)S(1)}, bf16[1,128,3072]{2,1,0:T(8,128)(2,1)S(1)}) custom-call(bf16[1,1,2,2,3072]{4,3,2,1,0:T(2,128)(2,1)} %x_ref.1, bf16[1,1,2,2,3072]{4,3,2,1,0:T(2,128)(2,1)} %cot_ref.1, s32[2,1,2]{2,1,0:T(1,128)} %counts_hbm.1, ...), custom_call_target="tpu_custom_call" | custom-call | tf_op jit(solution)/shard_map/expert_backward/pallas_call | solution.py:374
  32.3 1.5 %write_outputs.1 = (bf16[1,1,2,2,3072]{4,3,2,1,0:T(2,128)(2,1)}, bf16[1,3072,128]{2,1,0:T(8,128)(2,1)}, bf16[1,3072,128]{2,1,0:T(8,128)(2,1)}, bf16[1,128,3072]{2,1,0:T(8,128)(2,1)}) custom-call(bf16[32,384]{1,0:T(8,128)(2,1)S(1)} %get-tuple-element.8.final_ref, bf16[1,3072,128]{2,1,0:T(8,128)(2,1)S(1)} %get-tuple-element.9.gate_ref, ...), custom_call_target="tpu_custom_call" | custom-call | tf_op jit(solution)/shard_map/write_outputs/pallas_call | solution.py:408

commit v4 on v3

--- a/solution.py
+++ b/solution.py
@@ -79,8 +79,8 @@
     x_ref, cot_ref, counts_hbm, kept_ref, rank_ref, wg_ref, wu_ref, wd_ref,
     final_out, gate_out, up_out, down_out,
     slots, counts_ref,
-    stage, landed, rows, w_in, w_down, acc_gu, acc_dh, sib_out, sib_in, part, regroup, unit, unit_in,
-    s1_send, s1_recv, z_send, z_recv, y_send, y_recv, sb_send, sb_recv,
+    stage, pieces, rows, w_in, w_down, acc_gu, acc_dh, sib_out, sib_in, part, regroup, unit, unit_in,
+    z_send, z_recv, y_send, y_recv, sb_send, sb_recv,
     r1_send, r1_recv, r2_send, r2_recv, load_sem, slot_sem,
 ):
     s = lax.axis_index("expert")
@@ -100,11 +100,7 @@
             device_id_type=pl.DeviceIdType.MESH,
         )
 
-    near = [(0, 1), (1, 0), (1, 1)]
     others = [(de, dz, dy) for dz in (2, 3, 1, 0) for de in (1, 0) for dy in (1, 0) if (de, dz, dy) != (0, 0, 0)]
-
-    def near_device(de, dc):
-        return device((s + de) % 2, z, y, (c + dc) % 2)
 
     def other_device(de, dz, dy):
         return device((s + de) % 2, (z + dz) % 4, (y + dy) % 2, c)
@@ -120,7 +116,7 @@
         pltpu.make_async_copy(wd_ref.at[0], w_down, load_sem.at[2]),
     ]
     barrier = pltpu.get_barrier_semaphore()
-    greeted = [near_device(0, 1), near_device(1, 1)] + [other_device(*other) for other in others]
+    greeted = [device(s, z, y, 1 - c)] + [other_device(*other) for other in others]
     for where in greeted:
         pl.semaphore_signal(barrier, inc=1, device_id=where, device_id_type=pl.DeviceIdType.MESH)
     for load in slot_loads + loads:
@@ -128,57 +124,48 @@
     for load in slot_loads:
         load.wait()
 
-    row16 = lax.broadcasted_iota(jnp.int32, (16, quarter), 0)
-    slot = (row16 >> 2) & 1
+    row8 = lax.broadcasted_iota(jnp.int32, (8, quarter), 0)
     for e in range(2):
         live = jnp.where(s == 0, counts_ref[0, 0, e], counts_ref[1, 0, e])
-        sources = [slots[0, e].astype(jnp.float32), slots[1, e].astype(jnp.float32)]
-        for h in range(2):
-            value = jnp.zeros((16, quarter), jnp.float32)
-            for r in range(16):
-                t, k, g = r // 8, (r // 4) % 2, r % 4
-                start = h * half + g * quarter
-                line = sources[t][k:k + 1, start:start + quarter]
-                value = jnp.where(row16 == r, jnp.broadcast_to(line, value.shape), value)
-            stage[e, h] = jnp.where(slot < live, value, 0.0).astype(jnp.bfloat16)
-
-    i = lax.broadcasted_iota(jnp.int32, (64, 64), 0)
-    j = lax.broadcasted_iota(jnp.int32, (64, 64), 1)
+        for t in range(2):
+            source = slots[t, e].astype(jnp.float32)
+            groups = []
+            for k in range(2):
+                value = jnp.zeros((8, quarter), jnp.float32)
+                for g in range(8):
+                    line = source[k:k + 1, g * quarter:(g + 1) * quarter]
+                    value = jnp.where(row8 == g, jnp.broadcast_to(line, value.shape), value)
+                groups.append(value * jnp.where(k < live, 1.0, 0.0).astype(jnp.float32))
+            stage[e, t * 16:(t + 1) * 16, :] = jnp.concatenate(groups, axis=0).astype(jnp.bfloat16)
+
+    i = lax.broadcasted_iota(jnp.int32, (256, 256), 0)
+    j = lax.broadcasted_iota(jnp.int32, (256, 256), 1)
     order = (
-        ((i >> 4) == (j & 3))
-        & (((i >> 3) & 1) == ((j >> 3) & 1))
-        & (((i >> 2) & 1) == ((j >> 5) & 1))
-        & (((i >> 1) & 1) == ((j >> 4) & 1))
-        & ((i & 1) == ((j >> 2) & 1))
+        ((i >> 5) == (j & 7))
+        & (((i >> 4) & 1) == ((j >> 4) & 1))
+        & (((i >> 2) & 3) == (j >> 6))
+        & (((i >> 1) & 1) == ((j >> 5) & 1))
+        & ((i & 1) == ((j >> 3) & 1))
     ).astype(jnp.float32).astype(jnp.bfloat16)
 
     pl.semaphore_wait(barrier, len(greeted))
 
-    mine = pl.ds(pl.multiple_of((c * 2 + s) * 16, 16), 16)
     sends = []
-    first = []
-    for de, dc in near:
-        index = de * 2 + dc
+
+    def piece(ss, zz, yy, cc):
+        return pieces.at[yy * 2 + cc, pl.ds(pl.multiple_of((zz * 2 + ss) * 32, 32), 32), :]
+
+    line = [(1, 0), (0, 1), (1, 1), (0, 3), (1, 3), (0, 2), (1, 2)]
+    z_copies = {}
+    for de, dz in reversed(line):
+        index = de * 4 + dz
         copy = remote(
-            stage.at[(s + de) % 2, (c + dc) % 2], landed.at[mine, :], s1_send.at[index], s1_recv.at[index],
-            near_device(de, dc),
+            stage.at[(s + de) % 2], piece(s, z, y, c), z_send.at[index], z_recv.at[index], other_device(de, dz, 0)
         )
         copy.start()
-        first.append(copy)
-    landed[mine, :] = stage[s, c]
-    for copy in first:
-        copy.wait_recv()
-    sends += first
-
-    def block(zz, yy, hh):
-        return rows.at[
-            pl.ds(pl.multiple_of((yy * 4 + zz) * 16, 16), 16), pl.ds(pl.multiple_of(hh * half, 128), half)
-        ]
-
-    ordered = jnp.dot(order, landed[...], preferred_element_type=jnp.float32).astype(jnp.bfloat16)
-    my_rows = pl.ds(pl.multiple_of((y * 4 + z) * 16, 16), 16)
-    for g in range(4):
-        rows[my_rows, pl.ds(pl.multiple_of(c * half + g * quarter, 128), quarter)] = ordered[g * 16:(g + 1) * 16, :]
+        z_copies[de, dz] = copy
+        sends.append(copy)
+    pieces[y * 2 + c, pl.ds(pl.multiple_of((z * 2 + s) * 32, 32), 32), :] = stage[s]
 
     def forward(ref, send, recv, where):
         copy = remote(ref, ref, send, recv, where)
@@ -188,32 +175,34 @@
 
     sibling = device(s, z, y, 1 - c)
     opposite = device(s, z, 1 - y, c)
-    own = block(z, y, c)
-    z_copies = {}
-    for dz in (2, 1, 3):
-        z_copies[dz] = forward(own, z_send.at[dz - 1], z_recv.at[dz - 1], device(s, (z + dz) % 4, y, c))
-    y_copies = [forward(own, y_send.at[0], y_recv.at[0], opposite)]
-    s_copies = [forward(own, sb_send.at[0], sb_recv.at[0], sibling)]
-    for dz in (1, 3, 2):
-        z_copies[dz].wait_recv()
-        got = block((z + 4 - dz) % 4, y, c)
-        y_copies.append(forward(got, y_send.at[dz], y_recv.at[dz], opposite))
-        s_copies.append(forward(got, sb_send.at[dz], sb_recv.at[dz], sibling))
+    y_copies, s_copies = [], []
+    for de, dz in [(0, 0)] + line:
+        if (de, dz) != (0, 0):
+            z_copies[de, dz].wait_recv()
+        index = de * 4 + dz
+        got = piece((s + de) % 2, (z + 4 - dz) % 4, y, c)
+        y_copies.append(forward(got, y_send.at[index], y_recv.at[index], opposite))
+        s_copies.append(forward(got, sb_send.at[index], sb_recv.at[index], sibling))
 
     for load in loads:
         load.wait()
 
-    def forward_part(yy, hh, start):
-        columns = pl.ds(pl.multiple_of(hh * half, 256), half)
-        some = rows[pl.ds(pl.multiple_of(yy * 64, 64), 64), columns]
-        both = jnp.dot(some, w_in[columns, :], preferred_element_type=jnp.float32)
+    def arrange(yy, cc):
+        ordered = jnp.dot(order, pieces[yy * 2 + cc], preferred_element_type=jnp.float32).astype(jnp.bfloat16)
+        place = pl.ds(pl.multiple_of((yy * 2 + cc) * 32, 32), 32)
+        for g in range(8):
+            rows[place, g * quarter:(g + 1) * quarter] = ordered[g * 32:(g + 1) * 32, :]
+
+    def forward_part(yy, start, stop):
+        some = rows[pl.ds(pl.multiple_of(yy * 64, 64), 64), start:stop]
+        both = jnp.dot(some, w_in[start:stop, :], preferred_element_type=jnp.float32)
         back = lax.dot_general(
-            some, w_down[:, columns], (((1,), (1,)), ((), ())), preferred_element_type=jnp.float32
+            some, w_down[:, start:stop], (((1,), (1,)), ((), ())), preferred_element_type=jnp.float32
         )
-        both = both.reshape(4, 16, 256)[:, 0:8].reshape(32, 256)
-        back = back.reshape(4, 16, 128)[:, 8:16].reshape(32, 128)
+        both = both.reshape(2, 32, 256)[:, 0:16].reshape(32, 256)
+        back = back.reshape(2, 32, 128)[:, 16:32].reshape(32, 128)
         place = pl.ds(pl.multiple_of(yy * 32, 32), 32)
-        if not start:
+        if start > 0:
             both = both + acc_gu[place, :]
             back = back + acc_dh[place, :]
         acc_gu[place, :] = both
@@ -221,22 +210,28 @@
 
     last = []
 
-    def pass_on(n, dz):
+    def pass_on(n):
         y_copies[n].wait_recv()
-        got = block((z + 4 - dz) % 4, 1 - y, c)
-        last.append(forward(got, sb_send.at[4 + dz], sb_recv.at[4 + dz], sibling))
-
-    forward_part(y, c, True)
-    pass_on(0, 0)
+        de, dz = ([(0, 0)] + line)[n]
+        got = piece((s + de) % 2, (z + 4 - dz) % 4, 1 - y, c)
+        index = 8 + de * 4 + dz
+        last.append(forward(got, sb_send.at[index], sb_recv.at[index], sibling))
+
+    arrange(y, c)
+    for n in range(4):
+        pass_on(n)
     for copy in s_copies:
         copy.wait_recv()
-    forward_part(y, 1 - c, False)
-    for n, dz in ((1, 1), (2, 3), (3, 2)):
-        pass_on(n, dz)
-    forward_part(1 - y, c, True)
+    arrange(y, 1 - c)
+    forward_part(y, 0, half)
+    for n in range(4, 8):
+        pass_on(n)
+    arrange(1 - y, c)
+    forward_part(y, half, width)
     for copy in last:
         copy.wait_recv()
-    forward_part(1 - y, 1 - c, False)
+    arrange(1 - y, 1 - c)
+    forward_part(1 - y, 0, width)
 
     keep = jnp.where(rank_ref[0, 0] < kept_ref[0], 1.0, 0.0).astype(jnp.float32)
     gate_pre = acc_gu[:, 0:128]
@@ -253,9 +248,9 @@
     si = lax.broadcasted_iota(jnp.int32, (64, 64), 0)
     sj = lax.broadcasted_iota(jnp.int32, (64, 64), 1)
     split = (
-        ((sj >> 3) == ((si & 31) >> 2))
-        & ((sj & 3) == (si & 3))
-        & (((sj >> 2) & 1) == jnp.where(si >= 32, c, 1 - c))
+        ((sj >> 5) == ((si & 31) >> 4))
+        & ((sj & 15) == (si & 15))
+        & (((sj >> 4) & 1) == jnp.where(si >= 32, c, 1 - c))
     ).astype(jnp.float32).astype(jnp.bfloat16)
     by_core = jnp.dot(split, both_bf16, preferred_element_type=jnp.float32).astype(jnp.bfloat16)
     sib_copies = []
@@ -270,10 +265,10 @@
         part[n] = term[32:64]
     sends += sib_copies
 
-    zeros = jnp.zeros((8, 8, 128), jnp.float32)
-    hidden_pad = jnp.concatenate([zeros, hidden.reshape(8, 8, 128)], axis=1).reshape(128, 128).astype(jnp.bfloat16)
-    zeros2 = jnp.zeros((8, 8, 256), jnp.float32)
-    both_pad = jnp.concatenate([both_grad.reshape(8, 8, 256), zeros2], axis=1).reshape(128, 256).astype(jnp.bfloat16)
+    zeros = jnp.zeros((4, 16, 128), jnp.float32)
+    hidden_pad = jnp.concatenate([zeros, hidden.reshape(4, 16, 128)], axis=1).reshape(128, 128).astype(jnp.bfloat16)
+    zeros2 = jnp.zeros((4, 16, 256), jnp.float32)
+    both_pad = jnp.concatenate([both_grad.reshape(4, 16, 256), zeros2], axis=1).reshape(128, 256).astype(jnp.bfloat16)
 
     ui = lax.broadcasted_iota(jnp.int32, (256, 256), 0)
     uj = lax.broadcasted_iota(jnp.int32, (256, 256), 1)
@@ -384,8 +379,8 @@
         scratch_shapes=[
             pltpu.VMEM((2,) + x_rows.shape[2:], bf16),
             pltpu.SMEM(counts.shape, jnp.int32),
-            pltpu.VMEM((2, 2, 16, quarter), bf16),
-            pltpu.VMEM((64, quarter), bf16),
+            pltpu.VMEM((2, 32, quarter), bf16),
+            pltpu.VMEM((4, 256, quarter), bf16),
             pltpu.VMEM((128, width), bf16),
             pltpu.VMEM((width, 256), bf16),
             pltpu.VMEM((128, width), bf16),
@@ -397,7 +392,7 @@
             pltpu.VMEM((256, quarter), bf16),
             pltpu.VMEM((256, quarter), bf16),
             pltpu.VMEM((16, 16, quarter), bf16),
-            dma((4,)), dma((4,)), dma((3,)), dma((3,)), dma((4,)), dma((4,)), dma((8,)), dma((8,)),
+            dma((8,)), dma((8,)), dma((8,)), dma((8,)), dma((16,)), dma((16,)),
             dma((4,)), dma((4,)), dma((16,)), dma((16,)), dma((3,)), dma((3,)),
         ],
         compiler_params=pltpu.CompilerParams(

time: 34 us -> 30.9 us (0.909)
  Pallas kernels: 31.9 us -> 28.8 us
    pallas_call x1, Pallas kernels: 30.4 us -> 27.3 us  [kernel_body(): pl.pallas_call(exchange_kernel, out_shape=(jax.ShapeDtypeStruct((32, quar...]
where the time goes in v4:
time: 30.9 us; the launch traced here: 30.7 us
  Pallas kernels  28.8 us (93%)
  between operations  1.93 us (6%)
    pallas_call x1, Pallas kernels, kernel_body(): pl.pallas_call(exchange_kernel, out_shape=(jax.ShapeDtypeStruct((32, quar...  27.3 us
    pallas_call x1, Pallas kernels, kernel_body(): pl.pallas_call(finish_kernel, out_shape=tuple((jax.ShapeDtypeStruct(a.sha...  1.5 us

profile of v4, /device:TPU:0, one launch (start us, length us, event | category | flops | bytes accessed | tf_op | source)
XLA Modules:
  0.0 30.7 jit_solution(11471903508439163757)
XLA Ops:
  1.9 27.3 %expert_backward.1 = (bf16[32,384]{1,0:T(8,128)(2,1)S(1)}, bf16[1,3072,128]{2,1,0:T(8,128)(2,1)S(1)}, bf16[1,3072,128]{2,1,0:T(8,128)(2,1)S(1)}, bf16[1,128,3072]{2,1,0:T(8,128)(2,1)S(1)}) custom-call(bf16[1,1,2,2,3072]{4,3,2,1,0:T(2,128)(2,1)} %x_ref.1, bf16[1,1,2,2,3072]{4,3,2,1,0:T(2,128)(2,1)} %cot_ref.1, s32[2,1,2]{2,1,0:T(1,128)} %counts_hbm.1, ...), custom_call_target="tpu_custom_call" | custom-call | tf_op jit(solution)/shard_map/expert_backward/pallas_call | solution.py:369
  29.2 1.5 %write_outputs.1 = (bf16[1,1,2,2,3072]{4,3,2,1,0:T(2,128)(2,1)}, bf16[1,3072,128]{2,1,0:T(8,128)(2,1)}, bf16[1,3072,128]{2,1,0:T(8,128)(2,1)}, bf16[1,128,3072]{2,1,0:T(8,128)(2,1)}) custom-call(bf16[32,384]{1,0:T(8,128)(2,1)S(1)} %get-tuple-element.8.final_ref, bf16[1,3072,128]{2,1,0:T(8,128)(2,1)S(1)} %get-tuple-element.9.gate_ref, ...), custom_call_target="tpu_custom_call" | custom-call | tf_op jit(solution)/shard_map/write_outputs/pallas_call | solution.py:403

commit v5 on v4

--- a/solution.py
+++ b/solution.py
@@ -79,7 +79,7 @@
     x_ref, cot_ref, counts_hbm, kept_ref, rank_ref, wg_ref, wu_ref, wd_ref,
     final_out, gate_out, up_out, down_out,
     slots, counts_ref,
-    stage, pieces, rows, w_in, w_down, acc_gu, acc_dh, sib_out, sib_in, part, regroup, unit, unit_in,
+    stage, pieces, order, split, spread, rows, w_in, w_down, acc_gu, acc_dh, sib_out, sib_in, part, regroup, unit, unit_in,
     z_send, z_recv, y_send, y_recv, sb_send, sb_recv,
     r1_send, r1_recv, r2_send, r2_recv, load_sem, slot_sem,
 ):
@@ -138,16 +138,6 @@
                 groups.append(value * jnp.where(k < live, 1.0, 0.0).astype(jnp.float32))
             stage[e, t * 16:(t + 1) * 16, :] = jnp.concatenate(groups, axis=0).astype(jnp.bfloat16)
 
-    i = lax.broadcasted_iota(jnp.int32, (256, 256), 0)
-    j = lax.broadcasted_iota(jnp.int32, (256, 256), 1)
-    order = (
-        ((i >> 5) == (j & 7))
-        & (((i >> 4) & 1) == ((j >> 4) & 1))
-        & (((i >> 2) & 3) == (j >> 6))
-        & (((i >> 1) & 1) == ((j >> 5) & 1))
-        & ((i & 1) == ((j >> 3) & 1))
-    ).astype(jnp.float32).astype(jnp.bfloat16)
-
     pl.semaphore_wait(barrier, len(greeted))
 
     sends = []
@@ -155,9 +145,21 @@
     def piece(ss, zz, yy, cc):
         return pieces.at[yy * 2 + cc, pl.ds(pl.multiple_of((zz * 2 + ss) * 32, 32), 32), :]
 
+    def forward(ref, send, recv, where):
+        copy = remote(ref, ref, send, recv, where)
+        copy.start()
+        sends.append(copy)
+        return copy
+
+    sibling = device(s, z, y, 1 - c)
+    opposite = device(s, z, 1 - y, c)
+    own_rows = pl.ds(pl.multiple_of((z * 2 + s) * 32, 32), 32)
+    pieces[y * 2 + c, own_rows, :] = stage[s]
+    own = piece(s, z, y, c)
+    y_copies = [forward(own, y_send.at[0], y_recv.at[0], opposite)]
     line = [(1, 0), (0, 1), (1, 1), (0, 3), (1, 3), (0, 2), (1, 2)]
     z_copies = {}
-    for de, dz in reversed(line):
+    for de, dz in line[:1] + line[:0:-1]:
         index = de * 4 + dz
         copy = remote(
             stage.at[(s + de) % 2], piece(s, z, y, c), z_send.at[index], z_recv.at[index], other_device(de, dz, 0)
@@ -165,20 +167,33 @@
         copy.start()
         z_copies[de, dz] = copy
         sends.append(copy)
-    pieces[y * 2 + c, pl.ds(pl.multiple_of((z * 2 + s) * 32, 32), 32), :] = stage[s]
-
-    def forward(ref, send, recv, where):
-        copy = remote(ref, ref, send, recv, where)
-        copy.start()
-        sends.append(copy)
-        return copy
-
-    sibling = device(s, z, y, 1 - c)
-    opposite = device(s, z, 1 - y, c)
-    y_copies, s_copies = [], []
-    for de, dz in [(0, 0)] + line:
-        if (de, dz) != (0, 0):
-            z_copies[de, dz].wait_recv()
+    s_copies = [forward(own, sb_send.at[0], sb_recv.at[0], sibling)]
+
+    i = lax.broadcasted_iota(jnp.int32, (256, 256), 0)
+    j = lax.broadcasted_iota(jnp.int32, (256, 256), 1)
+    order[...] = (
+        ((i >> 5) == (j & 7))
+        & (((i >> 4) & 1) == ((j >> 4) & 1))
+        & (((i >> 2) & 3) == (j >> 6))
+        & (((i >> 1) & 1) == ((j >> 5) & 1))
+        & ((i & 1) == ((j >> 3) & 1))
+    ).astype(jnp.float32).astype(jnp.bfloat16)
+    si = lax.broadcasted_iota(jnp.int32, (64, 64), 0)
+    sj = lax.broadcasted_iota(jnp.int32, (64, 64), 1)
+    split[...] = (
+        ((sj >> 5) == ((si & 31) >> 4))
+        & ((sj & 15) == (si & 15))
+        & (((sj >> 4) & 1) == jnp.where(si >= 32, c, 1 - c))
+    ).astype(jnp.float32).astype(jnp.bfloat16)
+    spread[...] = (
+        ((j >> 5) == ((i >> 1) & 7))
+        & ((j & 1) == (i & 1))
+        & (((j >> 1) & 1) == ((i >> 4) & 1))
+        & (((j >> 2) & 7) == (i >> 5))
+    ).astype(jnp.float32).astype(jnp.bfloat16)
+
+    for de, dz in line:
+        z_copies[de, dz].wait_recv()
         index = de * 4 + dz
         got = piece((s + de) % 2, (z + 4 - dz) % 4, y, c)
         y_copies.append(forward(got, y_send.at[index], y_recv.at[index], opposite))
@@ -188,7 +203,7 @@
         load.wait()
 
     def arrange(yy, cc):
-        ordered = jnp.dot(order, pieces[yy * 2 + cc], preferred_element_type=jnp.float32).astype(jnp.bfloat16)
+        ordered = jnp.dot(order[...], pieces[yy * 2 + cc], preferred_element_type=jnp.float32).astype(jnp.bfloat16)
         place = pl.ds(pl.multiple_of((yy * 2 + cc) * 32, 32), 32)
         for g in range(8):
             rows[place, g * quarter:(g + 1) * quarter] = ordered[g * 32:(g + 1) * 32, :]
@@ -245,14 +260,7 @@
     both_grad = jnp.concatenate([gate_grad, up_grad], axis=1)
     both_bf16 = both_grad.astype(jnp.bfloat16)
 
-    si = lax.broadcasted_iota(jnp.int32, (64, 64), 0)
-    sj = lax.broadcasted_iota(jnp.int32, (64, 64), 1)
-    split = (
-        ((sj >> 5) == ((si & 31) >> 4))
-        & ((sj & 15) == (si & 15))
-        & (((sj >> 4) & 1) == jnp.where(si >= 32, c, 1 - c))
-    ).astype(jnp.float32).astype(jnp.bfloat16)
-    by_core = jnp.dot(split, both_bf16, preferred_element_type=jnp.float32).astype(jnp.bfloat16)
+    by_core = jnp.dot(split[...], both_bf16, preferred_element_type=jnp.float32).astype(jnp.bfloat16)
     sib_copies = []
     for n in range(4):
         term = lax.dot_general(
@@ -270,20 +278,18 @@
     zeros2 = jnp.zeros((4, 16, 256), jnp.float32)
     both_pad = jnp.concatenate([both_grad.reshape(4, 16, 256), zeros2], axis=1).reshape(128, 256).astype(jnp.bfloat16)
 
-    ui = lax.broadcasted_iota(jnp.int32, (256, 256), 0)
-    uj = lax.broadcasted_iota(jnp.int32, (256, 256), 1)
-    spread = (
-        ((uj >> 5) == ((ui >> 1) & 7))
-        & ((uj & 1) == (ui & 1))
-        & (((uj >> 1) & 1) == ((ui >> 4) & 1))
-        & (((uj >> 2) & 7) == (ui >> 5))
-    ).astype(jnp.float32).astype(jnp.bfloat16)
+    for n in range(4):
+        columns = pl.ds(n * pair, pair)
+        down_out[0, :, columns] = lax.dot_general(
+            hidden_pad, rows[:, columns], (((0,), (0,)), ((), ())), preferred_element_type=jnp.float32
+        ).astype(jnp.bfloat16)
+
     for n in range(4):
         sib_copies[n].wait_recv()
         total = (part[n] + sib_in[n].astype(jnp.float32)).astype(jnp.bfloat16)
         regroup[n * 64:n * 64 + 32, :] = total[:, 0:quarter]
         regroup[n * 64 + 32:n * 64 + 64, :] = total[:, quarter:]
-    unit[...] = jnp.dot(spread, regroup[...], preferred_element_type=jnp.float32).astype(jnp.bfloat16)
+    unit[...] = jnp.dot(spread[...], regroup[...], preferred_element_type=jnp.float32).astype(jnp.bfloat16)
 
     def unit_of(ee, zz, yy):
         return unit.at[pl.ds(pl.multiple_of(((yy * 4 + zz) * 2 + ee) * 16, 16), 16), :]
@@ -302,9 +308,6 @@
     for n in range(4):
         columns = pl.ds(n * pair, pair)
         some = rows[:, columns]
-        down_out[0, :, columns] = lax.dot_general(
-            hidden_pad, some, (((0,), (0,)), ((), ())), preferred_element_type=jnp.float32
-        ).astype(jnp.bfloat16)
         inner = lax.dot_general(
             some, both_pad, (((0,), (0,)), ((), ())), preferred_element_type=jnp.float32
         ).astype(jnp.bfloat16)
@@ -381,6 +384,9 @@
             pltpu.SMEM(counts.shape, jnp.int32),
             pltpu.VMEM((2, 32, quarter), bf16),
             pltpu.VMEM((4, 256, quarter), bf16),
+            pltpu.VMEM((256, 256), bf16),
+            pltpu.VMEM((64, 64), bf16),
+            pltpu.VMEM((256, 256), bf16),
             pltpu.VMEM((128, width), bf16),
             pltpu.VMEM((width, 256), bf16),
             pltpu.VMEM((128, width), bf16),

time: 30.9 us -> 30.9 us (level)
  no operation moved by 1% of the time
where the time goes in v5:
time: 30.9 us; the launch traced here: 30.7 us
  Pallas kernels  28.8 us (93%)
  between operations  1.93 us (6%)
    pallas_call x1, Pallas kernels, kernel_body(): pl.pallas_call(exchange_kernel, out_shape=(jax.ShapeDtypeStruct((32, quar...  27.3 us
    pallas_call x1, Pallas kernels, kernel_body(): pl.pallas_call(finish_kernel, out_shape=tuple((jax.ShapeDtypeStruct(a.sha...  1.5 us

profile of v5, /device:TPU:0, one launch (start us, length us, event | category | flops | bytes accessed | tf_op | source)
XLA Modules:
  0.0 30.7 jit_solution(15955285803586943073)
XLA Ops:
  1.9 27.3 %expert_backward.1 = (bf16[32,384]{1,0:T(8,128)(2,1)S(1)}, bf16[1,3072,128]{2,1,0:T(8,128)(2,1)S(1)}, bf16[1,3072,128]{2,1,0:T(8,128)(2,1)S(1)}, bf16[1,128,3072]{2,1,0:T(8,128)(2,1)S(1)}) custom-call(bf16[1,1,2,2,3072]{4,3,2,1,0:T(2,128)(2,1)} %x_ref.1, bf16[1,1,2,2,3072]{4,3,2,1,0:T(2,128)(2,1)} %cot_ref.1, s32[2,1,2]{2,1,0:T(1,128)} %counts_hbm.1, ...), custom_call_target="tpu_custom_call" | custom-call | tf_op jit(solution)/shard_map/expert_backward/pallas_call | solution.py:372
  29.2 1.5 %write_outputs.1 = (bf16[1,1,2,2,3072]{4,3,2,1,0:T(2,128)(2,1)}, bf16[1,3072,128]{2,1,0:T(8,128)(2,1)}, bf16[1,3072,128]{2,1,0:T(8,128)(2,1)}, bf16[1,128,3072]{2,1,0:T(8,128)(2,1)}) custom-call(bf16[32,384]{1,0:T(8,128)(2,1)S(1)} %get-tuple-element.8.final_ref, bf16[1,3072,128]{2,1,0:T(8,128)(2,1)S(1)} %get-tuple-element.9.gate_ref, ...), custom_call_target="tpu_custom_call" | custom-call | tf_op jit(solution)/shard_map/write_outputs/pallas_call | solution.py:409

commit v6 on v5

--- a/solution.py
+++ b/solution.py
@@ -79,7 +79,7 @@
     x_ref, cot_ref, counts_hbm, kept_ref, rank_ref, wg_ref, wu_ref, wd_ref,
     final_out, gate_out, up_out, down_out,
     slots, counts_ref,
-    stage, pieces, order, split, spread, rows, w_in, w_down, acc_gu, acc_dh, sib_out, sib_in, part, regroup, unit, unit_in,
+    stage, pieces, order, split, spread, rows, w_in, w_turned, w_down, acc_gu, acc_dh, sib_out, sib_in, part, regroup, unit, unit_in,
     z_send, z_recv, y_send, y_recv, sb_send, sb_recv,
     r1_send, r1_recv, r2_send, r2_recv, load_sem, slot_sem,
 ):
@@ -192,15 +192,22 @@
         & (((j >> 2) & 7) == (i >> 5))
     ).astype(jnp.float32).astype(jnp.bfloat16)
 
-    for de, dz in line:
+    for load in loads:
+        load.wait()
+
+    def turn(n):
+        some = pl.ds(n * quarter, quarter)
+        w_turned[:, some] = w_in[some, 0:256].T
+        w_in[some, 256:384] = w_down[:, some].T
+
+    turn(0)
+    for n, (de, dz) in enumerate(line):
         z_copies[de, dz].wait_recv()
         index = de * 4 + dz
         got = piece((s + de) % 2, (z + 4 - dz) % 4, y, c)
         y_copies.append(forward(got, y_send.at[index], y_recv.at[index], opposite))
         s_copies.append(forward(got, sb_send.at[index], sb_recv.at[index], sibling))
-
-    for load in loads:
-        load.wait()
+        turn(n + 1)
 
     def arrange(yy, cc):
         ordered = jnp.dot(order[...], pieces[yy * 2 + cc], preferred_element_type=jnp.float32).astype(jnp.bfloat16)
@@ -210,12 +217,9 @@
 
     def forward_part(yy, start, stop):
         some = rows[pl.ds(pl.multiple_of(yy * 64, 64), 64), start:stop]
-        both = jnp.dot(some, w_in[start:stop, :], preferred_element_type=jnp.float32)
-        back = lax.dot_general(
-            some, w_down[:, start:stop], (((1,), (1,)), ((), ())), preferred_element_type=jnp.float32
-        )
-        both = both.reshape(2, 32, 256)[:, 0:16].reshape(32, 256)
-        back = back.reshape(2, 32, 128)[:, 16:32].reshape(32, 128)
+        out = jnp.dot(some, w_in[start:stop, :], preferred_element_type=jnp.float32)
+        both = out[:, 0:256].reshape(2, 32, 256)[:, 0:16].reshape(32, 256)
+        back = out[:, 256:384].reshape(2, 32, 128)[:, 16:32].reshape(32, 128)
         place = pl.ds(pl.multiple_of(yy * 32, 32), 32)
         if start > 0:
             both = both + acc_gu[place, :]
@@ -263,9 +267,7 @@
     by_core = jnp.dot(split[...], both_bf16, preferred_element_type=jnp.float32).astype(jnp.bfloat16)
     sib_copies = []
     for n in range(4):
-        term = lax.dot_general(
-            by_core, w_in[n * pair:(n + 1) * pair, :], (((1,), (1,)), ((), ())), preferred_element_type=jnp.float32
-        )
+        term = jnp.dot(by_core, w_turned[:, n * pair:(n + 1) * pair], preferred_element_type=jnp.float32)
         sib_out[n] = term[0:32].astype(jnp.bfloat16)
         copy = remote(sib_out.at[n], sib_in.at[n], r1_send.at[n], r1_recv.at[n], sibling)
         copy.start()
@@ -277,12 +279,6 @@
     hidden_pad = jnp.concatenate([zeros, hidden.reshape(4, 16, 128)], axis=1).reshape(128, 128).astype(jnp.bfloat16)
     zeros2 = jnp.zeros((4, 16, 256), jnp.float32)
     both_pad = jnp.concatenate([both_grad.reshape(4, 16, 256), zeros2], axis=1).reshape(128, 256).astype(jnp.bfloat16)
-
-    for n in range(4):
-        columns = pl.ds(n * pair, pair)
-        down_out[0, :, columns] = lax.dot_general(
-            hidden_pad, rows[:, columns], (((0,), (0,)), ((), ())), preferred_element_type=jnp.float32
-        ).astype(jnp.bfloat16)
 
     for n in range(4):
         sib_copies[n].wait_recv()
@@ -308,6 +304,9 @@
     for n in range(4):
         columns = pl.ds(n * pair, pair)
         some = rows[:, columns]
+        down_out[0, :, columns] = lax.dot_general(
+            hidden_pad, some, (((0,), (0,)), ((), ())), preferred_element_type=jnp.float32
+        ).astype(jnp.bfloat16)
         inner = lax.dot_general(
             some, both_pad, (((0,), (0,)), ((), ())), preferred_element_type=jnp.float32
         ).astype(jnp.bfloat16)
@@ -388,7 +387,8 @@
             pltpu.VMEM((64, 64), bf16),
             pltpu.VMEM((256, 256), bf16),
             pltpu.VMEM((128, width), bf16),
-            pltpu.VMEM((width, 256), bf16),
+            pltpu.VMEM((width, 384), bf16),
+            pltpu.VMEM((256, width), bf16),
             pltpu.VMEM((128, width), bf16),
             pltpu.VMEM((64, 256), f32),
             pltpu.VMEM((64, 128), f32),

time: 30.9 us -> 30.7 us (level)
  no operation moved by 1% of the time
where the time goes in v6:
time: 30.7 us; the launch traced here: 30.5 us
  Pallas kernels  28.6 us (93%)
  between operations  1.93 us (6%)
    pallas_call x1, Pallas kernels, kernel_body(): pl.pallas_call(exchange_kernel, out_shape=(jax.ShapeDtypeStruct((32, quar...  27.1 us
    pallas_call x1, Pallas kernels, kernel_body(): pl.pallas_call(finish_kernel, out_shape=tuple((jax.ShapeDtypeStruct(a.sha...  1.5 us

profile of v6, /device:TPU:0, one launch (start us, length us, event | category | flops | bytes accessed | tf_op | source)
XLA Modules:
  0.0 30.5 jit_solution(10953601158334267673)
XLA Ops:
  1.9 27.1 %expert_backward.1 = (bf16[32,384]{1,0:T(8,128)(2,1)S(1)}, bf16[1,3072,128]{2,1,0:T(8,128)(2,1)S(1)}, bf16[1,3072,128]{2,1,0:T(8,128)(2,1)S(1)}, bf16[1,128,3072]{2,1,0:T(8,128)(2,1)S(1)}) custom-call(bf16[1,1,2,2,3072]{4,3,2,1,0:T(2,128)(2,1)} %x_ref.1, bf16[1,1,2,2,3072]{4,3,2,1,0:T(2,128)(2,1)} %cot_ref.1, s32[2,1,2]{2,1,0:T(1,128)} %counts_hbm.1, ...), custom_call_target="tpu_custom_call" | custom-call | tf_op jit(solution)/shard_map/expert_backward/pallas_call | solution.py:371
  29.0 1.5 %write_outputs.1 = (bf16[1,1,2,2,3072]{4,3,2,1,0:T(2,128)(2,1)}, bf16[1,3072,128]{2,1,0:T(8,128)(2,1)}, bf16[1,3072,128]{2,1,0:T(8,128)(2,1)}, bf16[1,128,3072]{2,1,0:T(8,128)(2,1)}) custom-call(bf16[32,384]{1,0:T(8,128)(2,1)S(1)} %get-tuple-element.8.final_ref, bf16[1,3072,128]{2,1,0:T(8,128)(2,1)S(1)} %get-tuple-element.9.gate_ref, ...), custom_call_target="tpu_custom_call" | custom-call | tf_op jit(solution)/shard_map/write_outputs/pallas_call | solution.py:409

commit v7 on v6

--- a/solution.py
+++ b/solution.py
@@ -102,8 +102,11 @@
 
     others = [(de, dz, dy) for dz in (2, 3, 1, 0) for de in (1, 0) for dy in (1, 0) if (de, dz, dy) != (0, 0, 0)]
 
+    def partner(dz):
+        return [z, z + 1 - 2 * (z % 2), (z + 2) % 4, 3 - z][dz]
+
     def other_device(de, dz, dy):
-        return device((s + de) % 2, (z + dz) % 4, (y + dy) % 2, c)
+        return device((s + de) % 2, partner(dz), (y + dy) % 2, c)
 
     slot_loads = [
         pltpu.make_async_copy(x_ref.at[0, 0], slots.at[0], slot_sem.at[0]),
@@ -159,7 +162,7 @@
     y_copies = [forward(own, y_send.at[0], y_recv.at[0], opposite)]
     line = [(1, 0), (0, 1), (1, 1), (0, 3), (1, 3), (0, 2), (1, 2)]
     z_copies = {}
-    for de, dz in line[:1] + line[:0:-1]:
+    for de, dz in line:
         index = de * 4 + dz
         copy = remote(
             stage.at[(s + de) % 2], piece(s, z, y, c), z_send.at[index], z_recv.at[index], other_device(de, dz, 0)
@@ -204,7 +207,7 @@
     for n, (de, dz) in enumerate(line):
         z_copies[de, dz].wait_recv()
         index = de * 4 + dz
-        got = piece((s + de) % 2, (z + 4 - dz) % 4, y, c)
+        got = piece((s + de) % 2, partner(dz), y, c)
         y_copies.append(forward(got, y_send.at[index], y_recv.at[index], opposite))
         s_copies.append(forward(got, sb_send.at[index], sb_recv.at[index], sibling))
         turn(n + 1)
@@ -232,7 +235,7 @@
     def pass_on(n):
         y_copies[n].wait_recv()
         de, dz = ([(0, 0)] + line)[n]
-        got = piece((s + de) % 2, (z + 4 - dz) % 4, 1 - y, c)
+        got = piece((s + de) % 2, partner(dz), 1 - y, c)
         index = 8 + de * 4 + dz
         last.append(forward(got, sb_send.at[index], sb_recv.at[index], sibling))
 
@@ -294,7 +297,7 @@
     for de, dz, dy in others:
         index = de * 8 + dz * 2 + dy
         copy = remote(
-            unit_of((s + de) % 2, (z + dz) % 4, (y + dy) % 2), unit_in.at[index],
+            unit_of((s + de) % 2, partner(dz), (y + dy) % 2), unit_in.at[index],
             r2_send.at[index], r2_recv.at[index], other_device(de, dz, dy),
         )
         copy.start()

time: 30.7 us -> 30.4 us (level)
    pallas_call x1, Pallas kernels: 27.1 us -> 26.8 us  [kernel_body(): pl.pallas_call(exchange_kernel, out_shape=(jax.ShapeDtypeStruct((32, quar...]
where the time goes in v7:
time: 30.4 us; the launch traced here: 30.2 us
  Pallas kernels  28.3 us (93%)
  between operations  1.93 us (6%)
    pallas_call x1, Pallas kernels, kernel_body(): pl.pallas_call(exchange_kernel, out_shape=(jax.ShapeDtypeStruct((32, quar...  26.8 us
    pallas_call x1, Pallas kernels, kernel_body(): pl.pallas_call(finish_kernel, out_shape=tuple((jax.ShapeDtypeStruct(a.sha...  1.5 us

profile of v7, /device:TPU:0, one launch (start us, length us, event | category | flops | bytes accessed | tf_op | source)
XLA Modules:
  0.0 30.2 jit_solution(2823160271451136123)
XLA Ops:
  1.9 26.8 %expert_backward.1 = (bf16[32,384]{1,0:T(8,128)(2,1)S(1)}, bf16[1,3072,128]{2,1,0:T(8,128)(2,1)S(1)}, bf16[1,3072,128]{2,1,0:T(8,128)(2,1)S(1)}, bf16[1,128,3072]{2,1,0:T(8,128)(2,1)S(1)}) custom-call(bf16[1,1,2,2,3072]{4,3,2,1,0:T(2,128)(2,1)} %x_ref.1, bf16[1,1,2,2,3072]{4,3,2,1,0:T(2,128)(2,1)} %cot_ref.1, s32[2,1,2]{2,1,0:T(1,128)} %counts_hbm.1, ...), custom_call_target="tpu_custom_call" | custom-call | tf_op jit(solution)/shard_map/expert_backward/pallas_call | solution.py:374
  28.7 1.5 %write_outputs.1 = (bf16[1,1,2,2,3072]{4,3,2,1,0:T(2,128)(2,1)}, bf16[1,3072,128]{2,1,0:T(8,128)(2,1)}, bf16[1,3072,128]{2,1,0:T(8,128)(2,1)}, bf16[1,128,3072]{2,1,0:T(8,128)(2,1)}) custom-call(bf16[32,384]{1,0:T(8,128)(2,1)S(1)} %get-tuple-element.8.final_ref, bf16[1,3072,128]{2,1,0:T(8,128)(2,1)S(1)} %get-tuple-element.9.gate_ref, ...), custom_call_target="tpu_custom_call" | custom-call | tf_op jit(solution)/shard_map/write_outputs/pallas_call | solution.py:412
